TPU v7x, 256 devices: a whole 4x4x8 slice. The times are simulated.
256 devices in a mesh: context: 64 (over x, z, core), head: 4 (over y).
Axes of the slice: x: 4, y: 4, z: 8, core: 2. Of those that a mesh axis runs over, the one named last changes fastest.
Arguments:
- query_vec: float32 [8192, 4096], P('context', 'head'), may hold values from -6 to 6
- key_vec: float32 [8192, 4096], P('context', 'head'), may hold values from -6 to 6
- value_vec: float32 [8192, 4096], P('context', 'head'), may hold values from -6 to 6
- log_decay: float32 [8192, 4096], P('context', 'head'), may hold values from -0.9 to 0
- beta: float32 [8192, 32], P('context', 'head'), may hold values from 0.5 to 0.95
- latent: bfloat16 [8192, 512], P(('context', 'head')), may hold values from -8 to 8
- latent_query: bfloat16 [8192, 16384], P('context', 'head'), may hold values from -64 to 64
- w_uv: bfloat16 [512, 4096], P(None, 'head'), may hold values from -0.25 to 0.25
- doc_lengths: int32 [128], replicated, may hold values from 1 to 512, 8192 in all
Outputs:
- delta_out: float32 [8192, 4096], P('context', 'head')
- mla_out: bfloat16 [8192, 4096], P('context', 'head')
Inputs may be any that keep to these rules, and one draw needn't show every extreme that they name: `doc_lengths`: each document has 1 to 512 tokens, the lengths sum to 8192, and the longest has exactly 512.
All inputs are finite; a program needn't handle non-finite values.
Results may differ from a plain program's by a relative error of at most 0.006.
Values may be sent and summed in bfloat16 or wider, within the bound.
A program may use at most 192 MiB of HBM per device.

v0:
```python
import math

import jax
import jax.numpy as jnp
from jax import lax
from jax.sharding import PartitionSpec as P

SPAN = 4


UPPER_LIMIT = lax.Precision.HIGHEST
FAR = -1e30


def carried_in(shard, axis, join, neutral):
    place = lax.axis_index(axis)
    gathered = jax.tree.map(
        lambda a, kind: lax.all_gather(a.astype(kind), axis), shard, (jnp.bfloat16, jnp.bfloat16)
    )
    state = jax.tree.map(lambda a, e: jnp.zeros_like(a) + jnp.asarray(e, a.dtype), shard, neutral)

    def one(step, state):
        return join(
            state,
            jax.tree.map(
                lambda a, own: lax.dynamic_index_in_dim(a, step, 0, False).astype(own.dtype),
                gathered,
                shard,
            ),
        )

    return lax.fori_loop(0, place, one, state)


def from_behind(value, axis, steps):
    count = lax.axis_size(axis)
    first, last = (max(0, -steps), min(count, count - steps))
    return lax.ppermute(value, axis, [(source, source + steps) for source in range(first, last)])


def doc_starts(doc_lengths, positions):
    endings = jnp.cumsum(doc_lengths)
    beginnings = endings - doc_lengths
    covered = beginnings[None, :] <= positions[:, None]
    return jnp.max(jnp.where(covered, beginnings[None, :], -1), axis=1)


def unit_rows(matrix):
    return matrix * lax.rsqrt(jnp.sum(matrix * matrix, axis=-1, keepdims=True) + 1e-06)


def multiplied_result(left, right, form):
    return jnp.einsum(form, left, right, precision=UPPER_LIMIT)


def chain_pair(earlier, later):
    transition = multiplied_result(later[0], earlier[0], "hij,hjk->hik")
    carried = multiplied_result(later[0], earlier[1], "hij,hjk->hik") + later[1]
    return (transition, carried)


def delta_blocks(query_vec, key_vec, value_vec, log_decay, beta, token_start, positions):
    tok_rows = query_vec.shape[0]
    head_count = beta.shape[1]
    key_width = query_vec.shape[1] // head_count
    value_width = value_vec.shape[1] // head_count
    block_len = math.gcd(tok_rows, 64)
    block_count = tok_rows // block_len

    def blocked(matrix, width):
        return matrix.reshape(block_count, block_len, head_count, width).transpose(0, 2, 1, 3)

    unit_query = unit_rows(blocked(query_vec, key_width))
    unit_key = unit_rows(blocked(key_vec, key_width))
    values_in = blocked(value_vec, value_width)
    cum_decay = jnp.cumsum(blocked(log_decay, key_width), axis=2)
    growth = jnp.exp(cum_decay)
    shrink = jnp.exp(-cum_decay)
    beta_col = beta.reshape(block_count, block_len, head_count).transpose(0, 2, 1)[..., None]
    segment = token_start.reshape(block_count, block_len)
    restart = (token_start == positions).reshape(block_count, block_len)
    same_doc = segment[:, :, None] == segment[:, None, :]
    order_idx = jnp.arange(block_len, dtype=jnp.int32)
    below_diag = order_idx[:, None] > order_idx[None, :]
    on_diag = order_idx[:, None] == order_idx[None, :]
    strict_mask = (same_doc & below_diag)[:, None]
    incl_mask = (same_doc & (below_diag | on_diag))[:, None]
    linked = (segment == segment[:, :1]) & jnp.logical_not(restart[:, :1])
    link_col = linked[:, None, :, None].astype(jnp.float32)
    link_last = linked[:, -1].astype(jnp.float32)[:, None, None, None]
    tail_col = same_doc[:, -1, :][:, None, :, None].astype(jnp.float32)
    key_grow = unit_key * growth
    key_shrink = unit_key * shrink
    lower_mat = (
        jnp.where(strict_mask, multiplied_result(key_grow, key_shrink, "nhtc,nhsc->nhts"), 0.0)
        * beta_col
    )
    system = lower_mat + jnp.eye(block_len, dtype=jnp.float32)
    right_side = beta_col * jnp.concatenate([values_in, key_grow * link_col], axis=-1)
    solved = lax.linalg.triangular_solve(
        system, right_side, left_side=True, lower=True, unit_diagonal=True
    )
    plain_part = solved[..., :value_width]
    absorbed = solved[..., value_width:]
    end_grow = growth[:, :, -1, :]
    key_tail = key_shrink * end_grow[:, :, None, :] * tail_col
    transition = jnp.eye(key_width, dtype=jnp.float32) * (
        end_grow[..., None] * link_last
    ) - multiplied_result(key_tail, absorbed, "nhsi,nhsj->nhij")
    carried = multiplied_result(key_tail, plain_part, "nhsi,nhsj->nhij")
    query_grow = unit_query * growth
    pair_weight = jnp.where(
        incl_mask, multiplied_result(query_grow, key_shrink, "nhtc,nhsc->nhts"), 0.0
    )
    query_left = query_grow * link_col - multiplied_result(pair_weight, absorbed, "nhts,nhsj->nhtj")
    query_base = multiplied_result(pair_weight, plain_part, "nhts,nhsj->nhtj")
    identity = (
        jnp.broadcast_to(jnp.eye(key_width, dtype=jnp.float32), (head_count, key_width, key_width)),
        jnp.zeros((head_count, key_width, value_width), jnp.float32),
    )

    def compose(running, inputs):
        return (chain_pair(running, inputs), None)

    shard_map_pair, _ = lax.scan(compose, identity, (transition, carried))
    return (shard_map_pair, identity, (transition, carried, query_left, query_base))


def delta_emit(incoming, pieces, tok_rows):

    def emit(present_state, inputs):
        step_trans, step_carried, remaining_stride, stride_starting = inputs
        produced_output = (
            multiplied_result(remaining_stride, present_state, "rcu,ruo->rco") + stride_starting
        )
        return (
            multiplied_result(step_trans, present_state, "hij,hjk->hik") + step_carried,
            produced_output,
        )

    _, produced_output = lax.scan(emit, incoming, pieces)
    head_count = produced_output.shape[1]
    value_width = produced_output.shape[3]
    return produced_output.transpose(0, 2, 1, 3).reshape(tok_rows, head_count * value_width)


def shards(query_vec, key_vec, value_vec, log_decay, beta, latent, latent_query, w_uv, doc_lengths):
    tok_rows = query_vec.shape[0]
    head_count = beta.shape[1]
    key_width = query_vec.shape[1] // head_count
    rank_width = w_uv.shape[0]
    value_width = w_uv.shape[1] // head_count
    shard_idx = lax.axis_index("context")
    shard_low = shard_idx * tok_rows
    shard_high = shard_low + tok_rows
    positions = shard_low + jnp.arange(tok_rows, dtype=jnp.int32)
    token_start = doc_starts(doc_lengths, positions)
    shard_pair, identity, pieces = delta_blocks(
        query_vec, key_vec, value_vec, log_decay, beta, token_start, positions
    )
    prefix = carried_in(
        (shard_pair[0], shard_pair[1]), "context", chain_pair, (identity[0], identity[1])
    )
    incoming = prefix[1]
    delta_out = delta_emit(incoming, pieces, tok_rows)
    keys_here = lax.all_gather(latent, "head", axis=0, tiled=True)
    query_rows = latent_query.reshape(tok_rows * head_count, rank_width)
    scale = key_width ** (-0.5)
    reach_low = shard_low - SPAN * tok_rows + 1

    def absorb_keys(running, key_rows, first_row):
        key_count = key_rows.shape[0]
        key_pos = first_row + jnp.arange(key_count, dtype=jnp.int32)
        key_doc = doc_starts(doc_lengths, key_pos)
        visible = (token_start[:, None] == key_doc[None, :]) & (
            key_pos[None, :] <= positions[:, None]
        )

        def update(carry_in):
            row_top, totals, summed = carry_in
            scores = jnp.einsum(
                "qr,kr->qk", query_rows, key_rows, preferred_element_type=jnp.float32
            )
            scores = scores.reshape(tok_rows, head_count, key_count) * scale
            scores = jnp.where(visible[:, None, :], scores, FAR)
            new_top = jnp.maximum(row_top, jnp.max(scores, axis=-1))
            weights = jnp.where(visible[:, None, :], jnp.exp(scores - new_top[..., None]), 0.0)
            fading = jnp.exp(row_top - new_top)
            totals = totals * fading + jnp.sum(weights, axis=-1)
            added = jnp.einsum(
                "qk,kr->qr",
                weights.astype(jnp.bfloat16).reshape(tok_rows * head_count, key_count),
                key_rows,
                preferred_element_type=jnp.float32,
            )
            summed = summed * fading[..., None] + added.reshape(tok_rows, head_count, rank_width)
            return (new_top, totals, summed)

        in_reach = (first_row + key_count > reach_low) & (first_row < shard_high)
        return lax.cond(in_reach, update, lambda carry_in: carry_in, running)

    initial = (
        jnp.full((tok_rows, head_count), FAR, jnp.float32),
        jnp.zeros((tok_rows, head_count), jnp.float32),
        jnp.zeros((tok_rows, head_count, rank_width), jnp.float32),
    )
    running = absorb_keys(initial, keys_here, shard_low)
    for distance in range(1, SPAN + 1):
        earlier = from_behind(keys_here, "context", distance)
        running = absorb_keys(running, earlier, shard_low - distance * tok_rows)
    context_vec = (running[2] / running[1][..., None]).astype(jnp.bfloat16)
    up_proj = w_uv.reshape(rank_width, head_count, value_width)
    mixed = jnp.einsum("thr,rhd->thd", context_vec, up_proj, preferred_element_type=jnp.float32)
    mla_out = mixed.astype(jnp.bfloat16).reshape(tok_rows, head_count * value_width)
    return (delta_out, mla_out)


def solution(mesh):
    return jax.shard_map(
        shards,
        mesh=mesh,
        in_specs=(
            P("context", "head"),
            P("context", "head"),
            P("context", "head"),
            P("context", "head"),
            P("context", "head"),
            P(("context", "head"), None),
            P("context", "head"),
            P(None, "head"),
            P(),
        ),
        out_specs=(P("context", "head"), P("context", "head")),
        check_vma=False,
    )
```

profile of v0, /device:TPU:231, one launch (start us, length us, event | category | flops | bytes accessed | tf_op | source)
XLA Modules:
  0.0 427.8 jit_solution(7252929582790763448)
XLA Ops:
  10.9 13.0 %fusion.61 = f32[2,8,64,128]{3,1,2,0:T(8,128)S(1)} fusion(f32[2,64,8,128]{3,2,1,0:T(8,128)S(1)} %bitcast.230), kind=kOutput, calls=%fused_computation.107 | output fusion | flops 8257536 | bytes 1048576 | tf_op jit(solution)/shard_map/jit(cumsum)/reduce_window_sum | solution.py:76
  25.9 1.9 fusion.57
  27.8 79.4 %custom-call.3 = f32[2,8,1,64,64]{3,4,2,1,0:T(8,128)S(1)} custom-call(f32[2,8,1,64,64]{4,3,2,1,0:T(8,128)} %fusion.57), custom_call_target="InvertDiagBlocksLowerTriangular" | custom-call | tf_op jit(solution)/shard_map/triangular_solve | solution.py:100
  109.8 1.9 fusion.70
  111.7 2.1 convolution_subtract_fusion
  113.8 2.9 while.39
  118.4 10.4 %all_gather.19 = bf16[128,512]{1,0:T(8,128)(2,1)} all-gather(bf16[32,512]{1,0:T(8,128)(2,1)S(1)} %copy-done.13), channel_id=1, replica_groups=mesh['context'=64,'head'=4] {'head'}, dimensions={0}, use_global_device_ids=true | all-gather | bytes 163840 | tf_op jit(solution)/shard_map/all_gather | solution.py:166
  132.6 1.5 collective-permute-start.3
  134.2 2.4 reshape.353
  136.6 2.4 copy.78
  141.6 1.5 fusion.68
  143.0 1.7 convolution_subtract_fusion.1
  144.8 4.9 %conditional.5 = (f32[128,8]{1,0:T(8,128)}, f32[128,8]{1,0:T(8,128)S(1)}, f32[128,8,512]{2,0,1:T(8,128)S(1)}) conditional(s32[]{:T(128)} %convert_element_type.120, () %tuple.65, (pred[128,128]{1,0:T(8,128)(4,1)S(1)}, bf16[1024,512]{1,0:T(8,128)(2,1)S(1)}, bf16[128,512]{1,0:T(8,128)(2,1)}) %tuple.161), branch_computations={%region_11.12_spmd, %region_12.15_spmd} | conditional | flops 269879296 | bytes 5079064 | solution.py:200
  149.7 12.9 %conditional.6 = ((f32[128,8]{1,0:T(8,128)}, f32[128,8]{1,0:T(8,128)S(1)}, f32[128,8,512]{2,0,1:T(8,128)S(1)})) conditional(s32[]{:T(128)} %convert_element_type.119, (f32[128,8]{1,0:T(8,128)}, f32[128,8]{1,0:T(8,128)S(1)}, f32[128,8,512]{2,0,1:T(8,128)S(1)}) %conditional.5, (pred[128,128]{1,0:T(8,128)(4,1)S(1)}, bf16[1024,512]{1,0:T(8,128)(2,1)}, ...), branch_computations={%region_16.17_spmd, %region_17.20_spmd} | conditional | flops 270403584 | bytes 7270460 | solution.py:200
  149.8 2.5 fusion.89
  153.9 2.0 fusion.21
  157.3 1.5 multiply_add_fusion.1
  158.8 1.5 copy.54
  160.3 1.7 multiply_add_fusion
  162.7 12.3 %conditional.7 = ((f32[128,8]{1,0:T(8,128)}, f32[128,8]{1,0:T(8,128)S(1)}, f32[128,8,512]{2,0,1:T(8,128)S(1)})) conditional(s32[]{:T(128)} %convert_element_type.118, (f32[128,8]{1,0:T(8,128)}, f32[128,8]{1,0:T(8,128)S(1)}, f32[128,8,512]{2,0,1:T(8,128)S(1)}) %get-tuple-element.684, (pred[128,128]{1,0:T(8,128)(4,1)S(1)}, ...), branch_computations={%region_21.22_spmd, %region_22.25_spmd} | conditional | flops 270403584 | bytes 7204896 | solution.py:200
  162.7 2.5 fusion.90
  166.8 2.0 fusion.27
  170.1 1.5 multiply_add_fusion.3
  172.6 1.8 multiply_add_fusion.2
  178.2 14.2 %conditional.8 = ((f32[128,8]{1,0:T(8,128)}, f32[128,8]{1,0:T(8,128)S(1)}, f32[128,8,512]{2,0,1:T(8,128)S(1)})) conditional(s32[]{:T(128)} %convert_element_type.117, (f32[128,8]{1,0:T(8,128)}, f32[128,8]{1,0:T(8,128)S(1)}, f32[128,8,512]{2,0,1:T(8,128)S(1)}) %get-tuple-element.685, (s32[128]{0:T(128)}, s32[]{:T(128)}, s32[128,1]{0,1:T(1,128)S(1)}, ...), branch_computations={%region_25.26_spmd, %region_26.30_spmd} | conditional | flops 270502016 | bytes 7422504 | solution.py:200
  180.2 2.5 fusion.91
  184.3 2.0 fusion.33
  187.6 1.5 multiply_add_fusion.5
  190.0 1.8 multiply_add_fusion.4
  192.4 13.8 %conditional.9 = ((f32[128,8]{1,0:T(8,128)S(1)}, f32[128,8,512]{2,0,1:T(8,128)S(1)})) conditional(s32[]{:T(128)} %convert_element_type.116, (f32[128,8]{1,0:T(8,128)S(1)}, f32[128,8,512]{2,0,1:T(8,128)S(1)}) %tuple.70, (s32[128]{0:T(128)}, s32[]{:T(128)}, s32[128,1]{0,1:T(1,128)S(1)}, s32[128,128]{1,0:T(8,128)}, s32[128,128]{1,0:T(8,128)}, ...), branch_computations={%region_30.31_spmd, %region_31.35_spmd} | conditional | flops 270502016 | bytes 7414304 | solution.py:200
  194.4 2.5 fusion.92
  198.5 2.0 fusion.39
  201.9 1.5 multiply_add_fusion.7
  204.3 1.8 multiply_add_fusion.6
  206.3 1.8 convolution_convert_fusion
  208.9 8.5 %all-gather.5.cloned.1.call-done = bf16[512,128,128]{2,1,0:T(8,128)(2,1)} async-done(((bf16[8,128,128]{2,1,0:T(8,128)(2,1)}), bf16[512,128,128]{2,1,0:T(8,128)(2,1)}) %all-gather.5.cloned.1.call-update) | async-done | bytes 16777232 | tf_op jit(solution)/shard_map/all_gather | solution.py:18
  217.4 99.5 %all-gather.7.cloned.1.call-done = bf16[512,128,128]{2,1,0:T(8,128)(2,1)} async-done(((bf16[8,128,128]{2,1,0:T(8,128)(2,1)}), bf16[512,128,128]{2,1,0:T(8,128)(2,1)}) %all-gather.7.cloned.1.call-update) | async-done | bytes 16777232 | tf_op jit(solution)/shard_map/all_gather | solution.py:18
  317.0 95.8 %while.37 = (s32[]{:T(128)}, f32[8,128,128]{2,1,0:T(8,128)S(1)}, s32[]{:T(128)}, bf16[64,8,128,128]{3,2,1,0:T(8,128)(2,1)}, bf16[64,8,128,128]{3,2,1,0:T(8,128)(2,1)}, /*index=5*/s32[]{:T(128)}, s32[]{:T(128)}, s32[]{:T(128)}) while((s32[]{:T(128)}, f32[8,128,128]{2,1,0:T(8,128)S(1)}, s32[]{:T(128)}, bf16[64,8,128,128]{3,2,1,0:T(8,128)(2,1)}, ...), condition=%wide.region_7.8_spmd, body=%wide.region_6.7_spmd.sunk | while | flops 201588736 | bytes 2622583 | solution.py:32
  317.0 1.5 convolution_add_fusion.8
  323.2 1.4 convolution_add_fusion.8
  338.4 1.4 convolution_add_fusion.8
  353.6 1.4 convolution_add_fusion.8
  368.8 1.4 convolution_add_fusion.8
  376.4 1.4 convolution_add_fusion.8
  391.6 1.4 convolution_add_fusion.8
  412.8 5.9 %while.38 = (s32[]{:T(128)}, f32[8,128,128]{2,1,0:T(8,128)S(1)}, f32[2,8,64,128]{3,2,1,0:T(8,128)}, f32[2,8,128,128]{3,2,1,0:T(8,128)S(1)}, f32[2,8,128,128]{3,2...) while((s32[]{:T(128)}, f32[8,128,128]{2,1,0:T(8,128)S(1)}, ...), condition=%wide.region_10.11_spmd, body=%wide.region_9.10_spmd.sunk | while | flops 302186496 | bytes 4458581 | solution.py:141
  412.9 2.3 fusion.130
  415.8 2.3 fusion.130
  (275 shorter events, 135.2 us)
Async XLA Ops:
  7.2 16.8 %copy-start.10 = (f32[128,1024]{1,0:T(8,128)S(1)}, f32[128,1024]{1,0:T(8,128)}, u32[]{:S(2)}) copy-start(f32[128,1024]{1,0:T(8,128)} %param.26) | copy-start | bytes 1572868
  7.2 210.2 %all-gather.5.cloned.1.call-start = ((), (), s32[]{:S(2)}) async-start(), calls=%async_computation | async-start | bytes 17039360 | tf_op jit(solution)/shard_map/all_gather | solution.py:18
  7.2 137.5 %copy-start.14 = (s32[128]{0:T(128)}, s32[128]{0:T(128)S(1)}, u32[]{:S(2)}) copy-start(s32[128]{0:T(128)S(1)} %iota_add_fusion.3) | copy-start | bytes 1540
  8.2 16.4 %copy-start.17 = (f32[128,8]{0,1:T(8,128)S(1)}, f32[128,8]{0,1:T(8,128)}, u32[]{:S(2)}) copy-start(f32[128,8]{0,1:T(8,128)} %param.29) | copy-start | bytes 12292
  9.0 1.9 copy-start.16
  9.3 135.5 %copy-start.15 = (s32[128]{0:T(128)}, s32[128]{0:T(128)S(1)}, u32[]{:S(2)}) copy-start(s32[128]{0:T(128)S(1)} %get-tuple-element.401) | copy-start | bytes 1540
  24.0 1.9 copy-start.3
  24.8 82.4 %copy-start.11 = (f32[128,1024]{1,0:T(8,128)S(1)}, f32[128,1024]{1,0:T(8,128)}, u32[]{:S(2)}) copy-start(f32[128,1024]{1,0:T(8,128)} %param.27) | copy-start | bytes 1572868
  25.9 85.8 %copy-start.5 = (f32[2,8,64,128]{3,2,1,0:T(8,128)}, f32[2,8,64,128]{3,2,1,0:T(8,128)S(1)}, u32[]{:S(2)}) copy-start(f32[2,8,64,128]{3,2,1,0:T(8,128)S(1)} %get-tuple-element.471) | copy-start | bytes 1572868
  109.8 4.0 copy-start.7
  116.7 19.8 %copy-start.1 = (f32[2,8,128,128]{3,2,1,0:T(8,128)}, f32[2,8,128,128]{3,2,1,0:T(8,128)S(1)}, u32[]{:S(2)}) copy-start(f32[2,8,128,128]{3,2,1,0:T(8,128)S(1)} %get-tuple-element.695) | copy-start | bytes 3145732
  116.7 1.7 copy-start.13
  117.6 199.3 %all-gather.7.cloned.1.call-start = ((), (), s32[]{:S(2)}) async-start(), calls=%async_computation.1 | async-start | bytes 17039360 | tf_op jit(solution)/shard_map/all_gather | solution.py:18
  128.7 21.0 %collective-permute-start = (bf16[128,512]{1,0:T(8,128)(2,1)}, bf16[128,512]{1,0:T(8,128)(2,1)}, u32[]{:S(2)}, u32[]{:S(2)}) collective-permute-start(bf16[128,512]{1,0:T(8,128)(2,1)} %all_gather.19), channel_id=1, source_target_pairs={{0,4},{4,8},{8,12},{12,16},{16,20},{20,24},{24,28},{28,32},{32,36}... | collective-permute-start | bytes 393224 | tf_op jit(solution)/shard_map/ppermute | solution.py:38
  130.0 32.6 %collective-permute-start.1 = (bf16[128,512]{1,0:T(8,128)(2,1)}, bf16[128,512]{1,0:T(8,128)(2,1)}, u32[]{:S(2)}, u32[]{:S(2)}) collective-permute-start(bf16[128,512]{1,0:T(8,128)(2,1)} %all_gather.19), channel_id=1, source_target_pairs={{0,8},{4,12},{8,16},{12,20},{16,24},{20,28},{24,32},{28,36},{32,40... | collective-permute-start | bytes 393224 | tf_op jit(solution)/shard_map/ppermute | solution.py:38
  131.3 43.7 %collective-permute-start.2 = (bf16[128,512]{1,0:T(8,128)(2,1)}, bf16[128,512]{1,0:T(8,128)(2,1)}, u32[]{:S(2)}, u32[]{:S(2)}) collective-permute-start(bf16[128,512]{1,0:T(8,128)(2,1)} %all_gather.19), channel_id=1, source_target_pairs={{0,12},{4,16},{8,20},{12,24},{16,28},{20,32},{24,36},{28,40},{32,4... | collective-permute-start | bytes 393224 | tf_op jit(solution)/shard_map/ppermute | solution.py:38
  132.6 59.8 %collective-permute-start.3 = (bf16[128,512]{1,0:T(8,128)(2,1)}, bf16[128,512]{1,0:T(8,128)(2,1)}, u32[]{:S(2)}, u32[]{:S(2)}) collective-permute-start(bf16[128,512]{1,0:T(8,128)(2,1)} %all_gather.19), channel_id=1, source_target_pairs={{0,16},{4,20},{8,24},{12,28},{16,32},{20,36},{24,40},{28,44},{32,4... | collective-permute-start | bytes 393224 | tf_op jit(solution)/shard_map/ppermute | solution.py:38
  136.5 3.9 copy-start.4
  136.5 3.9 copy-start.6
  138.9 2.6 copy-start.8
  141.6 3.3 copy-start
  149.7 4.1 copy-start.12
  316.9 95.8 %copy-start.2 = (f32[2,8,128,128]{3,2,1,0:T(8,128)S(1)}, f32[2,8,128,128]{3,2,1,0:T(8,128)}, u32[]{:S(2)}) copy-start(f32[2,8,128,128]{3,2,1,0:T(8,128)} %copy-done.1) | copy-start | bytes 3145732
  316.9 95.8 %copy-start.9 = (f32[2,8,64,128]{3,2,1,0:T(8,128)S(1)}, f32[2,8,64,128]{3,2,1,0:T(8,128)}, u32[]{:S(2)}) copy-start(f32[2,8,64,128]{3,2,1,0:T(8,128)} %fusion.68) | copy-start | bytes 1572868
Sparse Core Ops, SparseCore 0:
  117.7 99.6 all-gather.4
  220.2 96.6 all-gather.6
where the time goes:
time: 431 us; the launch traced here: 428 us
  matrix products  132 us (31%)
  other arithmetic  120 us (28%)
  waiting for transfers between devices  108 us (25%)
  local copies, waits for them, and re-layouts  33.9 us (8%)
  between operations  14.6 us (3%)
  blocking collectives  10.4 us (2%)
  starting transfers between devices  5.42 us (1%)
    dot_general x77, matrix products, multiplied_result(): return jnp.einsum(form, left, right, precision=UPPER_LIMIT)  110 us
    all_gather x2, waiting for transfers between devices, carried_in(): lax.all_gather(a.astype(kind), axis)  108 us
    another operation x3, other arithmetic, delta_blocks(): lax.linalg.triangular_solve(system, right_side, left_side=True, lower=Tru...  79.4 us
    another operation x1, other arithmetic, delta_blocks(): cum_decay = jnp.cumsum(blocked(log_decay, key_width), axis=2)  13 us
    dot_general x5, matrix products, update(): jnp.einsum('qr,kr->qk', query_rows, key_rows, preferred_element_type=jnp....  11.3 us
    all_gather x1, blocking collectives, shards(): keys_here = lax.all_gather(latent, 'head', axis=0, tiled=True)  10.4 us
  transfers between devices with their start and end apart: 6, of which 2 were waited for; matrix products, arithmetic and copies ran while one was open for 18% of the time, Pallas kernels for 0%

commit v1 on v0

v1 whole, which is shorter than its diff:
```python
import functools

import jax
import jax.numpy as jnp
from jax import lax
from jax.experimental import pallas as pl
from jax.experimental.pallas import tpu as pltpu
from jax.sharding import PartitionSpec as P

MESH = pl.DeviceIdType.MESH
F32 = jnp.float32
BF16 = jnp.bfloat16
FAR = -1e30
EPS = 1e-6
SPAN = 4
TOK = 128
WIDTH = 128
GROUP = 4
LEVELS = 7


def mul(left, right):
    return lax.dot_general(left, right, (((1,), (0,)), ((), ())), preferred_element_type=F32)


def mul_nt(left, right):
    return lax.dot_general(left, right, (((1,), (1,)), ((), ())), preferred_element_type=F32)


def mul_tn(left, right):
    return lax.dot_general(left, right, (((0,), (0,)), ((), ())), preferred_element_type=F32)


def halves(matrix):
    high = matrix.astype(BF16)
    return high, (matrix - high.astype(F32)).astype(BF16)


def three(product, left, right):
    return product(left[0], right[0]) + product(left[1], right[0]) + product(left[0], right[1])


def iota2(shape, axis):
    return lax.broadcasted_iota(jnp.int32, shape, axis)


def prepare_masks(lens, shard, pair_mask, link_mask, level_mask, bias):
    square = (TOK, TOK)
    row, col = iota2(square, 0), iota2(square, 1)
    lens_f = lens.astype(F32)
    lens_row = jnp.broadcast_to(lens_f, square)
    begin_col = jnp.sum(jnp.where(col < row, lens_row, 0.0), axis=1, keepdims=True)
    lens_col = jnp.sum(jnp.where(col == row, lens_row, 0.0), axis=1, keepdims=True)
    begin_row = jnp.sum(jnp.where(row < col, lens_col, 0.0), axis=0, keepdims=True)
    low = shard * TOK
    pos_col = (low + iota2((TOK, 1), 0)).astype(F32)
    start_col = jnp.max(jnp.where(begin_row <= pos_col, begin_row, -1.0), axis=1, keepdims=True)
    keys = (SPAN + 1) * TOK
    pos_row = (low - SPAN * TOK + iota2((1, keys), 1)).astype(F32)
    start_row = jnp.max(jnp.where(begin_col <= pos_row, begin_col, -1.0), axis=0, keepdims=True)
    visible = (start_col == start_row) & (pos_row <= pos_col)
    bias[...] = jnp.where(visible, 0.0, FAR)
    same = start_col == start_row[:, SPAN * TOK :]
    pair_mask[0] = jnp.where(same & (row >= col), 1.0, 0.0)
    pair_mask[1] = jnp.where(same & (row > col), 1.0, 0.0)
    link_mask[0] = jnp.broadcast_to(jnp.where(start_col < low.astype(F32), 1.0, 0.0), square)
    link_mask[1] = jnp.broadcast_to(jnp.where(start_col == start_col[TOK - 1 :, :], 1.0, 0.0), square)
    for level in range(LEVELS):
        below = ((row >> (level + 1)) == (col >> (level + 1))) & ((row >> level) > (col >> level))
        level_mask[level] = jnp.where(below, 1.0, 0.0).astype(BF16)
    level_mask[LEVELS] = jnp.where(row == col, 1.0, 0.0).astype(BF16)


def delta_local(first, heads, refs, pair_mask, link_mask, level_mask, a_ref, c_ref, left_ref, base_ref):
    query_ref, key_ref, value_ref, decay_ref, beta_ref = refs
    square = (TOK, TOK)
    row, col = iota2(square, 0), iota2(square, 1)
    lower = jnp.where(row >= col, 1.0, 0.0).astype(BF16)
    incl, strict = pair_mask[0] > 0.5, pair_mask[1] > 0.5
    link, tail = link_mask[0], link_mask[1]
    link_last = link[TOK - 1 :, :]
    beta_all = beta_ref[...]
    beta_col = iota2(beta_all.shape, 1)
    span = range(heads)
    lanes = [pl.ds(pl.multiple_of((first + h) * WIDTH, WIDTH), WIDTH) for h in span]
    solve, weight, q_in, tail_t, right, end_row = [], [], [], [], [], []
    for h in span:
        decay = decay_ref[:, lanes[h]]
        high, rest = decay.astype(BF16), None
        rest = decay - high.astype(F32)
        mid = rest.astype(BF16)
        low = (rest - mid.astype(F32)).astype(BF16)
        cum = mul(lower, high) + mul(lower, mid) + mul(lower, low)
        centre, end = cum[TOK // 2 - 1 : TOK // 2, :], cum[TOK - 1 :, :]
        grow, shrink = jnp.exp(cum - centre), jnp.exp(centre - cum)
        from_start, to_end = jnp.exp(centre), jnp.exp(end - centre)
        query, key = query_ref[:, lanes[h]], key_ref[:, lanes[h]]
        query = query * lax.rsqrt(jnp.sum(query * query, axis=1, keepdims=True) + EPS)
        key = key * lax.rsqrt(jnp.sum(key * key, axis=1, keepdims=True) + EPS)
        query_grow, key_grow, key_shrink = query * grow, key * grow, key * shrink
        pairs = three(
            mul_nt, halves(jnp.concatenate([query_grow, key_grow], axis=0)), halves(key_shrink)
        )
        beta = jnp.sum(jnp.where(beta_col == first + h, beta_all, 0.0), axis=1, keepdims=True)
        weight.append(halves(jnp.where(incl, pairs[:TOK], 0.0)))
        solve.append(halves(jnp.where(strict, pairs[TOK:], 0.0) * beta))
        in_scale = link * from_start
        q_in.append(query_grow * in_scale)
        right.append(
            jnp.concatenate([value_ref[:, lanes[h]] * beta, key_grow * in_scale * beta], axis=1)
        )
        tail_t.append(halves(key_shrink * (tail * to_end)))
        end_row.append(jnp.exp(end) * link_last)
    inverse = [level_mask[LEVELS] - solve[h][0] * level_mask[0] for h in span]
    for level in range(1, LEVELS):
        part = [mul(solve[h][0] * level_mask[level], inverse[h]).astype(BF16) for h in span]
        inverse = [inverse[h] - mul(inverse[h], part[h]).astype(BF16) for h in span]
    solved = [mul(inverse[h], right[h].astype(BF16)) for h in span]
    rest = [right[h] - solved[h] - three(mul, solve[h], halves(solved[h])) for h in span]
    solved = [halves(solved[h] + mul(inverse[h], rest[h].astype(BF16))) for h in span]
    for h in span:
        change = three(mul_tn, tail_t[h], solved[h])
        output = three(mul, weight[h], solved[h])
        c_ref[first + h] = change[:, :WIDTH]
        a_ref[first + h] = (jnp.where(row == col, end_row[h], 0.0) - change[:, WIDTH:]).astype(BF16)
        base_ref[:, lanes[h]] = output[:, :WIDTH]
        left_ref[first + h] = (q_in[h] - output[:, WIDTH:]).astype(BF16)


def latent_part(first, heads, scale, query_rows, keys, bias, up_ref, out_ref):
    rows = heads * TOK
    scores = mul_nt(query_rows[first * TOK : first * TOK + rows, :], keys[...])
    mask = jnp.concatenate([bias[...]] * heads, axis=0)
    scores = scores * scale + mask
    top = jnp.max(scores, axis=1, keepdims=True)
    weights = jnp.exp(scores - top)
    totals = jnp.sum(weights, axis=1, keepdims=True)
    context = mul(weights.astype(BF16), keys[...]) * (1.0 / totals)
    context = context.astype(BF16)
    for h in range(heads):
        at = (first + h) * WIDTH
        out_ref[:, at : at + WIDTH] = mul(
            context[h * TOK : (h + 1) * TOK], up_ref[:, at : at + WIDTH]
        ).astype(BF16)


def body(
    shards, head_devices, heads, scale,
    query_hbm, key_hbm, value_hbm, decay_hbm, beta_ref, latent_hbm, latq_hbm, up_hbm, lens_ref,
    delta_hbm, mla_hbm,
    query_v, key_v, value_v, decay_v, latq_v, up_v, keys, base, mla_v,
    pair_mask, link_mask, level_mask, bias,
    a_ref, c_ref, left_ref, send_buf, recv_buf,
    load_sem, store_sem, chain_send, chain_recv, near_send, near_recv, side_send, side_recv, twin_send, twin_recv,
):
    shard = lax.axis_index("context")
    side = lax.axis_index("head")
    core = lax.rem(shard, 2)
    rank = latq_v.shape[1]
    quarter = TOK // head_devices

    def behind(steps):
        return lax.rem(shard + shards + steps, shards)

    def block_rows(block, place):
        return pl.ds(pl.multiple_of(block * TOK + place * quarter, quarter), quarter)

    loads = [
        pltpu.make_async_copy(source, target, load_sem.at[i])
        for i, (source, target) in enumerate(
            [(decay_hbm, decay_v), (key_hbm, key_v), (query_hbm, query_v), (value_hbm, value_v), (up_hbm, up_v)]
        )
    ]
    for h in range(heads):
        loads.append(
            pltpu.make_async_copy(
                latq_hbm.at[:, pl.ds(h * rank, rank)], latq_v.at[pl.ds(h * TOK, TOK), :], load_sem.at[5 + h]
            )
        )
    own = pltpu.make_async_copy(latent_hbm, keys.at[block_rows(SPAN, side)], load_sem.at[5 + heads])
    own.start()
    for load in loads:
        load.start()

    barrier = pltpu.get_barrier_semaphore()
    peers = [(behind(steps), side) for steps in (1, -1, 2, -2, 4, -4)]
    peers += [(shard, lax.rem(side + step, head_devices)) for step in range(1, head_devices)]
    for peer in peers:
        pl.semaphore_signal(barrier, inc=1, device_id=peer, device_id_type=MESH)
    pl.semaphore_wait(barrier, len(peers))

    def near_copy(i):
        steps = (2, 4)[i]
        return pltpu.make_async_remote_copy(
            src_ref=latent_hbm, dst_ref=keys.at[block_rows(SPAN - steps, side)],
            send_sem=near_send.at[i], recv_sem=near_recv.at[i],
            device_id=(behind(steps), side), device_id_type=MESH,
        )

    def side_copy(i, step):
        place = block_rows(SPAN - 2 * i, side)
        at = i * (head_devices - 1) + step - 1
        return pltpu.make_async_remote_copy(
            src_ref=keys.at[place], dst_ref=keys.at[place],
            send_sem=side_send.at[at], recv_sem=side_recv.at[at],
            device_id=(shard, lax.rem(side + step, head_devices)), device_id_type=MESH,
        )

    def side_arrival(i, step):
        place = block_rows(SPAN - 2 * i, lax.rem(side + head_devices - step, head_devices))
        at = i * (head_devices - 1) + step - 1
        return pltpu.make_async_remote_copy(
            src_ref=keys.at[place], dst_ref=keys.at[place],
            send_sem=side_send.at[at], recv_sem=side_recv.at[at],
            device_id=(shard, lax.rem(side + step, head_devices)), device_id_type=MESH,
        )

    def twin_copy(i):
        source = pl.ds(pl.multiple_of((2 * i + 2 * (1 - core)) * TOK, TOK), TOK)
        return pltpu.make_async_remote_copy(
            src_ref=keys.at[source], dst_ref=keys.at[pl.ds((2 * i + 1) * TOK, TOK)],
            send_sem=twin_send.at[i], recv_sem=twin_recv.at[i],
            device_id=(shard + 1 - 2 * core, side), device_id_type=MESH,
        )

    def chain_copy(step, h):
        return pltpu.make_async_remote_copy(
            src_ref=send_buf.at[step, h], dst_ref=recv_buf.at[step, h],
            send_sem=chain_send.at[step, h], recv_sem=chain_recv.at[step, h],
            device_id=(behind(1), side), device_id_type=MESH,
        )

    def chain_first(first, count):
        @pl.when(core == 0)
        def _():
            for h in range(first, first + count):
                send_buf[0, h] = c_ref[h].astype(BF16)
                chain_copy(0, h).start()

    def chain_second(first, count):
        @pl.when(core == 1)
        def _():
            for h in range(first, first + count):
                chain_copy(0, h).wait_recv()
                joined = c_ref[h] + mul(a_ref[h], recv_buf[0, h])
                c_ref[h] = joined
                send_buf[0, h] = joined.astype(BF16)
                chain_copy(0, h).start()

    def chain_third(first, count):
        @pl.when(core == 0)
        def _():
            for h in range(first, first + count):
                chain_copy(0, h).wait_recv()
                send_buf[1, h] = mul(a_ref[h], recv_buf[0, h]).astype(BF16)
                chain_copy(1, h).start()

    def chain_fourth(first, count):
        @pl.when(core == 1)
        def _():
            for h in range(first, first + count):
                chain_copy(1, h).wait_recv()
                send_buf[1, h] = (c_ref[h] + mul(a_ref[h], recv_buf[1, h])).astype(BF16)
                chain_copy(1, h).start()

    def emit(h, incoming):
        at = h * WIDTH
        base[:, at : at + WIDTH] += mul(left_ref[h], incoming)

    def chain_fifth(first, count):
        @pl.when(core == 0)
        def _():
            for h in range(first, first + count):
                chain_copy(1, h).wait_recv()
                send_buf[2, h] = (c_ref[h] + mul(a_ref[h], recv_buf[1, h])).astype(BF16)
                chain_copy(2, h).start()
                emit(h, recv_buf[1, h])

    def chain_sixth(first, count):
        @pl.when(core == 1)
        def _():
            for h in range(first, first + count):
                chain_copy(2, h).wait_recv()
                emit(h, recv_buf[2, h])

    for i in range(2):
        near_copy(i).start()
    own.wait()
    for step in range(1, head_devices):
        side_copy(0, step).start()

    prepare_masks(lens_ref[...], shard, pair_mask, link_mask, level_mask, bias)
    for load in loads[:4]:
        load.wait()
    refs = (query_v, key_v, value_v, decay_v, beta_ref)
    delta_local(0, GROUP, refs, pair_mask, link_mask, level_mask, a_ref, c_ref, left_ref, base)
    chain_first(0, GROUP)
    for i in range(2):
        near_copy(i).wait_recv()
        for step in range(1, head_devices):
            side_copy(i + 1, step).start()
    delta_local(GROUP, GROUP, refs, pair_mask, link_mask, level_mask, a_ref, c_ref, left_ref, base)
    chain_first(GROUP, GROUP)
    chain_second(0, heads)
    for i in range(SPAN // 2 + 1):
        for step in range(1, head_devices):
            side_arrival(i, step).wait_recv()
    for i in range(2):
        twin_copy(i).start()
    for load in loads[4:]:
        load.wait()
    for i in range(2):
        twin_copy(i).wait_recv()

    def latent_at(part):
        latent_part(part * 2, 2, scale, latq_v, keys, bias, up_v, mla_v)

    latent_at(0)
    chain_third(0, heads)
    latent_at(1)
    chain_fourth(0, heads)
    latent_at(2)
    chain_fifth(0, heads)
    latent_at(3)
    mla_out = pltpu.make_async_copy(mla_v, mla_hbm, store_sem.at[0])
    mla_out.start()
    chain_sixth(0, heads)
    delta_out = pltpu.make_async_copy(base, delta_hbm, store_sem.at[1])
    delta_out.start()
    for i in range(2):
        near_copy(i).wait_send()
        twin_copy(i).wait_send()
    for i in range(SPAN // 2 + 1):
        for step in range(1, head_devices):
            side_copy(i, step).wait_send()
    for h in range(heads):
        for step in range(2):
            chain_copy(step, h).wait_send()

    @pl.when(core == 0)
    def _():
        for h in range(heads):
            chain_copy(2, h).wait_send()

    mla_out.wait()
    delta_out.wait()


def solution(mesh):
    shards = mesh.shape["context"]
    head_devices = mesh.shape["head"]

    def step(query_vec, key_vec, value_vec, log_decay, beta, latent, latent_query, w_uv, doc_lengths):
        rows = query_vec.shape[0]
        heads = beta.shape[1]
        rank = w_uv.shape[0]
        width = query_vec.shape[1]
        keys = (SPAN + 1) * rows
        square = (rows, rows)
        anywhere = pl.BlockSpec(memory_space=pl.ANY)
        inside = pl.BlockSpec(memory_space=pltpu.VMEM)
        dma = pltpu.SemaphoreType.DMA
        side_copies = (SPAN // 2 + 1) * (head_devices - 1)
        return pl.pallas_call(
            functools.partial(body, shards, head_devices, heads, WIDTH**-0.5),
            out_shape=(
                jax.ShapeDtypeStruct((rows, width), F32),
                jax.ShapeDtypeStruct((rows, width), BF16),
            ),
            in_specs=[anywhere] * 4 + [inside] + [anywhere] * 3 + [inside],
            out_specs=(anywhere, anywhere),
            scratch_shapes=[
                pltpu.VMEM((rows, width), F32),
                pltpu.VMEM((rows, width), F32),
                pltpu.VMEM((rows, width), F32),
                pltpu.VMEM((rows, width), F32),
                pltpu.VMEM((rows * heads, rank), BF16),
                pltpu.VMEM((rank, width), BF16),
                pltpu.VMEM((keys, rank), BF16),
                pltpu.VMEM((rows, width), F32),
                pltpu.VMEM((rows, width), BF16),
                pltpu.VMEM((2,) + square, F32),
                pltpu.VMEM((2,) + square, F32),
                pltpu.VMEM((LEVELS + 1,) + square, BF16),
                pltpu.VMEM((rows, keys), F32),
                pltpu.VMEM((heads,) + square, BF16),
                pltpu.VMEM((heads,) + square, F32),
                pltpu.VMEM((heads,) + square, BF16),
                pltpu.VMEM((3, heads) + square, BF16),
                pltpu.VMEM((3, heads) + square, BF16),
                dma((6 + heads,)),
                dma((2,)),
                dma((3, heads)),
                dma((3, heads)),
                dma((2,)),
                dma((2,)),
                dma((side_copies,)),
                dma((side_copies,)),
                dma((2,)),
                dma((2,)),
            ],
            compiler_params=pltpu.CompilerParams(
                collective_id=0, has_side_effects=True, vmem_limit_bytes=48 * 1024 * 1024
            ),
            cost_estimate=pl.CostEstimate(flops=3_000_000_000, bytes_accessed=6_000_000, transcendentals=1_000_000),
            name="packed_attention",
        )(
            query_vec, key_vec, value_vec, log_decay, beta, latent, latent_query, w_uv,
            doc_lengths.reshape(1, -1),
        )

    return jax.shard_map(
        step,
        mesh=mesh,
        in_specs=(
            P("context", "head"),
            P("context", "head"),
            P("context", "head"),
            P("context", "head"),
            P("context", "head"),
            P(("context", "head"), None),
            P("context", "head"),
            P(None, "head"),
            P(),
        ),
        out_specs=(P("context", "head"), P("context", "head")),
        check_vma=False,
    )
```

time: 431 us -> 41.6 us (0.10)
  the two profiles are of different devices: /device:TPU:231 before, /device:TPU:1 now
where the time goes in v1:
time: 41.6 us; the launch traced here: 41.2 us
  Pallas kernels  31.6 us (76%)
  local copies, waits for them, and re-layouts  8.91 us (21%)
  between operations  0.68 us (2%)
    pallas_call x1, Pallas kernels, step(): pl.pallas_call(functools.partial(body, shards, head_devices, heads, WIDTH...  31.6 us
    unnamed x19, local copies, waits for them, and re-layouts  8.91 us

profile of v1, /device:TPU:1, one launch (start us, length us, event | category | flops | bytes accessed | tf_op | source)
XLA Modules:
  0.0 41.2 jit_solution(116902516388583890)
XLA Ops:
  0.6 0.0 copy-start.6
  0.6 0.0 copy-start.7
  0.7 0.8 %copy.11.beta_ref = f32[128,8]{1,0:T(8,128)S(1)} copy(f32[128,8]{0,1:T(8,128)} %param.13) | data formatting | bytes 8192 | tf_op args[4]
  1.4 0.0 copy-done.6
  1.5 0.0 copy-done.7
  1.5 0.0 copy-start
  1.5 1.2 %copy-done = bf16[128,4096]{1,0:T(8,128)(2,1)S(1)} copy-done((bf16[128,4096]{1,0:T(8,128)(2,1)S(1)}, bf16[128,4096]{1,0:T(8,128)(2,1)}, u32[]{:S(2)}) %copy-start) | copy-done | bytes 1048600
  2.7 0.0 copy-start.1
  2.7 1.2 %copy-done.1 = bf16[512,1024]{1,0:T(8,128)(2,1)S(1)} copy-done((bf16[512,1024]{1,0:T(8,128)(2,1)S(1)}, bf16[512,1024]{1,0:T(8,128)(2,1)}, u32[]{:S(2)}) %copy-start.1) | copy-done | bytes 1048600
  3.9 0.0 copy-start.2
  3.9 1.0 %copy-done.2 = f32[128,1024]{1,0:T(8,128)S(1)} copy-done((f32[128,1024]{1,0:T(8,128)S(1)}, f32[128,1024]{1,0:T(8,128)}, u32[]{:S(2)}) %copy-start.2) | copy-done | bytes 524312
  5.0 0.0 copy-start.3
  5.0 1.0 %copy-done.3 = f32[128,1024]{1,0:T(8,128)S(1)} copy-done((f32[128,1024]{1,0:T(8,128)S(1)}, f32[128,1024]{1,0:T(8,128)}, u32[]{:S(2)}) %copy-start.3) | copy-done | bytes 524312
  6.0 0.0 copy-start.4
  6.0 1.0 %copy-done.4 = f32[128,1024]{1,0:T(8,128)S(1)} copy-done((f32[128,1024]{1,0:T(8,128)S(1)}, f32[128,1024]{1,0:T(8,128)}, u32[]{:S(2)}) %copy-start.4) | copy-done | bytes 524312
  7.0 0.0 copy-start.5
  7.0 1.0 %copy-done.5 = f32[128,1024]{1,0:T(8,128)S(1)} copy-done((f32[128,1024]{1,0:T(8,128)S(1)}, f32[128,1024]{1,0:T(8,128)}, u32[]{:S(2)}) %copy-start.5) | copy-done | bytes 524312
  8.1 31.6 %packed_attention.1 = (f32[128,1024]{1,0:T(8,128)S(1)}, bf16[128,1024]{1,0:T(8,128)(2,1)S(1)}) custom-call(f32[128,1024]{1,0:T(8,128)S(1)} %copy-done.2, f32[128,1024]{1,0:T(8,128)S(1)} %copy-done.3, f32[128,1024]{1,0:T(8,128)S(1)} %copy-done.4, f32[128,1024]{1,0:T(8,128)S(1)} %copy-done.5, f32[128,8]{1,0:T(8,128)S(1)} %copy.11.beta_ref, ...), custom_call_target="tpu_custom_call" | custom-call | flops 3000000000 | bytes 6000000 | tf_op jit(solution)/shard_map/packed_attention/pallas_call | solution.py:364
  39.7 0.8 %copy.14 = f32[128,1024]{1,0:T(8,128)} copy(f32[128,1024]{1,0:T(8,128)S(1)} %get-tuple-element.4) | data formatting | bytes 1048576
  40.5 0.7 %copy.15 = bf16[128,1024]{1,0:T(8,128)(2,1)} copy(bf16[128,1024]{1,0:T(8,128)(2,1)S(1)} %get-tuple-element.5) | data formatting | bytes 524288
Async XLA Ops:
  0.6 0.8 %copy-start.6 = (bf16[32,512]{1,0:T(8,128)(2,1)S(1)}, bf16[32,512]{1,0:T(8,128)(2,1)}, u32[]{:S(2)}) copy-start(bf16[32,512]{1,0:T(8,128)(2,1)} %latent_hbm.1) | copy-start | bytes 98308
  0.6 0.8 %copy-start.7 = (s32[128]{0:T(128)S(1)}, s32[128]{0:T(128)}, u32[]{:S(2)}) copy-start(s32[128]{0:T(128)} %param.17) | copy-start | bytes 1540
  1.5 1.2 %copy-start = (bf16[128,4096]{1,0:T(8,128)(2,1)S(1)}, bf16[128,4096]{1,0:T(8,128)(2,1)}, u32[]{:S(2)}) copy-start(bf16[128,4096]{1,0:T(8,128)(2,1)} %latq_hbm.1) | copy-start | bytes 3145732
  2.7 1.2 %copy-start.1 = (bf16[512,1024]{1,0:T(8,128)(2,1)S(1)}, bf16[512,1024]{1,0:T(8,128)(2,1)}, u32[]{:S(2)}) copy-start(bf16[512,1024]{1,0:T(8,128)(2,1)} %up_hbm.1) | copy-start | bytes 3145732
  3.9 1.0 %copy-start.2 = (f32[128,1024]{1,0:T(8,128)S(1)}, f32[128,1024]{1,0:T(8,128)}, u32[]{:S(2)}) copy-start(f32[128,1024]{1,0:T(8,128)} %query_hbm.1) | copy-start | bytes 1572868
  5.0 1.0 %copy-start.3 = (f32[128,1024]{1,0:T(8,128)S(1)}, f32[128,1024]{1,0:T(8,128)}, u32[]{:S(2)}) copy-start(f32[128,1024]{1,0:T(8,128)} %key_hbm.1) | copy-start | bytes 1572868
  6.0 1.0 %copy-start.4 = (f32[128,1024]{1,0:T(8,128)S(1)}, f32[128,1024]{1,0:T(8,128)}, u32[]{:S(2)}) copy-start(f32[128,1024]{1,0:T(8,128)} %value_hbm.1) | copy-start | bytes 1572868
  7.0 1.0 %copy-start.5 = (f32[128,1024]{1,0:T(8,128)S(1)}, f32[128,1024]{1,0:T(8,128)}, u32[]{:S(2)}) copy-start(f32[128,1024]{1,0:T(8,128)} %decay_hbm.1) | copy-start | bytes 1572868

commit v2 on v1

v2 whole, which is shorter than its diff:
```python
import functools

import jax
import jax.numpy as jnp
from jax import lax
from jax.experimental import pallas as pl
from jax.experimental.pallas import tpu as pltpu
from jax.sharding import PartitionSpec as P

MESH = pl.DeviceIdType.MESH
F32 = jnp.float32
BF16 = jnp.bfloat16
FAR = -1e30
EPS = 1e-6
SPAN = 4
TOK = 128
WIDTH = 128
LEVELS = 7


def mul(left, right):
    return lax.dot_general(left, right, (((1,), (0,)), ((), ())), preferred_element_type=F32)


def mul_nt(left, right):
    return lax.dot_general(left, right, (((1,), (1,)), ((), ())), preferred_element_type=F32)


def mul_tn(left, right):
    return lax.dot_general(left, right, (((0,), (0,)), ((), ())), preferred_element_type=F32)


def halves(matrix):
    high = matrix.astype(BF16)
    return high, (matrix - high.astype(F32)).astype(BF16)


def three(product, left, right):
    return product(left[0], right[0]) + product(left[1], right[0]) + product(left[0], right[1])


def iota2(shape, axis):
    return lax.broadcasted_iota(jnp.int32, shape, axis)


def prepare_masks(lens, shard, pair_mask, link_mask, level_mask, bias):
    square = (TOK, TOK)
    row, col = iota2(square, 0), iota2(square, 1)
    lens_f = lens.astype(F32)
    lens_row = jnp.broadcast_to(lens_f, square)
    begin_col = jnp.sum(jnp.where(col < row, lens_row, 0.0), axis=1, keepdims=True)
    lens_col = jnp.sum(jnp.where(col == row, lens_row, 0.0), axis=1, keepdims=True)
    begin_row = jnp.sum(jnp.where(row < col, lens_col, 0.0), axis=0, keepdims=True)
    low = shard * TOK
    pos_col = (low + iota2((TOK, 1), 0)).astype(F32)
    start_col = jnp.max(jnp.where(begin_row <= pos_col, begin_row, -1.0), axis=1, keepdims=True)
    keys = (SPAN + 1) * TOK
    pos_row = (low - SPAN * TOK + iota2((1, keys), 1)).astype(F32)
    start_row = jnp.max(jnp.where(begin_col <= pos_row, begin_col, -1.0), axis=0, keepdims=True)
    visible = (start_col == start_row) & (pos_row <= pos_col)
    bias[...] = jnp.where(visible, 0.0, FAR)
    same = start_col == start_row[:, SPAN * TOK :]
    pair_mask[0] = jnp.where(same & (row >= col), 1.0, 0.0)
    pair_mask[1] = jnp.where(same & (row > col), 1.0, 0.0)
    link_mask[0] = jnp.broadcast_to(jnp.where(start_col < low.astype(F32), 1.0, 0.0), square)
    link_mask[1] = jnp.broadcast_to(jnp.where(start_col == start_col[TOK - 1 :, :], 1.0, 0.0), square)
    for level in range(LEVELS):
        below = ((row >> (level + 1)) == (col >> (level + 1))) & ((row >> level) > (col >> level))
        level_mask[level] = jnp.where(below, 1.0, 0.0).astype(BF16)
    level_mask[LEVELS] = jnp.where(row == col, 1.0, 0.0).astype(BF16)


def delta_pairs(heads, refs, pair_mask, link_mask):
    query_ref, key_ref, value_ref, decay_ref, beta_ref = refs
    square = (TOK, TOK)
    row, col = iota2(square, 0), iota2(square, 1)
    lower = jnp.where(row >= col, 1.0, 0.0).astype(BF16)
    incl, strict = pair_mask[0] > 0.5, pair_mask[1] > 0.5
    link, tail = link_mask[0], link_mask[1]
    link_last = link[TOK - 1 :, :]
    beta_cols = beta_ref[...].T
    parts = []
    for h in range(heads):
        lanes = slice(h * WIDTH, (h + 1) * WIDTH)
        decay = decay_ref[:, lanes]
        high = decay.astype(BF16)
        rest = decay - high.astype(F32)
        mid = rest.astype(BF16)
        low = (rest - mid.astype(F32)).astype(BF16)
        cum = mul(lower, high) + mul(lower, mid) + mul(lower, low)
        centre, end = cum[TOK // 2 - 1 : TOK // 2, :], cum[TOK - 1 :, :]
        grow, shrink = jnp.exp(cum - centre), jnp.exp(centre - cum)
        from_start, to_end = jnp.exp(centre), jnp.exp(end - centre)
        query, key = query_ref[:, lanes], key_ref[:, lanes]
        query = query * lax.rsqrt(jnp.sum(query * query, axis=1, keepdims=True) + EPS)
        key = key * lax.rsqrt(jnp.sum(key * key, axis=1, keepdims=True) + EPS)
        query_grow, key_grow, key_shrink = query * grow, key * grow, key * shrink
        pairs = three(
            mul_nt, halves(jnp.concatenate([query_grow, key_grow], axis=0)), halves(key_shrink)
        )
        beta = beta_cols[:, h : h + 1]
        in_scale = link * from_start
        parts.append(
            dict(
                weight=halves(jnp.where(incl, pairs[:TOK], 0.0)),
                system=halves(jnp.where(strict, pairs[TOK:], 0.0) * beta),
                query_in=query_grow * in_scale,
                right=jnp.concatenate(
                    [value_ref[:, lanes] * beta, key_grow * in_scale * beta], axis=1
                ),
                tail=halves(key_shrink * (tail * to_end)),
                end=jnp.exp(end) * link_last,
            )
        )
    return parts


def delta_solve(parts, level_mask, a_ref, c_ref):
    square = (TOK, TOK)
    row, col = iota2(square, 0), iota2(square, 1)
    system = [part["system"] for part in parts]
    right = [part["right"] for part in parts]
    span = range(len(parts))
    inverse = [level_mask[LEVELS] - system[h][0] * level_mask[0] for h in span]
    for level in range(1, LEVELS):
        inner = [mul(system[h][0] * level_mask[level], inverse[h]).astype(BF16) for h in span]
        inverse = [inverse[h] - mul(inverse[h], inner[h]).astype(BF16) for h in span]
    solved = [mul(inverse[h], right[h].astype(BF16)) for h in span]
    rest = [right[h] - solved[h] - three(mul, system[h], halves(solved[h])) for h in span]
    solved = [halves(solved[h] + mul(inverse[h], rest[h].astype(BF16))) for h in span]
    for h in span:
        change = three(mul_tn, parts[h]["tail"], solved[h])
        c_ref[h] = change[:, :WIDTH]
        a_ref[h] = (jnp.where(row == col, parts[h]["end"], 0.0) - change[:, WIDTH:]).astype(BF16)
    return solved


def delta_outputs(parts, solved, left_ref, base_ref):
    for h in range(len(parts)):
        output = three(mul, parts[h]["weight"], solved[h])
        base_ref[:, h * WIDTH : (h + 1) * WIDTH] = output[:, :WIDTH]
        left_ref[h] = (parts[h]["query_in"] - output[:, WIDTH:]).astype(BF16)


def latent_part(first, heads, scale, query_rows, keys, bias, up_ref, out_ref):
    rows = heads * TOK
    scores = mul_nt(query_rows[first * TOK : first * TOK + rows, :], keys[...])
    mask = jnp.concatenate([bias[...]] * heads, axis=0)
    scores = scores * scale + mask
    top = jnp.max(scores, axis=1, keepdims=True)
    weights = jnp.exp(scores - top)
    totals = jnp.sum(weights, axis=1, keepdims=True)
    context = mul(weights.astype(BF16), keys[...]) * (1.0 / totals)
    context = context.astype(BF16)
    for h in range(heads):
        at = (first + h) * WIDTH
        out_ref[:, at : at + WIDTH] = mul(
            context[h * TOK : (h + 1) * TOK], up_ref[:, at : at + WIDTH]
        ).astype(BF16)


def body(
    shards, head_devices, heads, scale,
    query_hbm, key_hbm, value_hbm, decay_hbm, beta_hbm, latent_hbm, latq_hbm, up_hbm, lens_hbm,
    base, mla_v,
    query_v, key_v, value_v, decay_v, beta_v, latq_v, up_v, keys, lens_v,
    pair_mask, link_mask, level_mask, bias,
    a_ref, c_ref, left_ref, step_ref, send_buf, recv_buf,
    load_sem, chain_send, chain_recv, near_send, near_recv, side_send, side_recv, twin_send, twin_recv,
):
    shard = lax.axis_index("context")
    side = lax.axis_index("head")
    core = lax.rem(shard, 2)
    chip = shard // 2
    last = shards // 2 - 1
    is_a, is_b = core == 0, core == 1
    rank = latq_v.shape[1]
    quarter = TOK // head_devices
    near = (2, 4)

    def ahead(steps):
        return lax.rem(shard + shards + steps, shards)

    def block_rows(block, place):
        return pl.ds(pl.multiple_of(block * TOK + place * quarter, quarter), quarter)

    pairs = [(lens_hbm, lens_v), (decay_hbm, decay_v), (key_hbm, key_v), (query_hbm, query_v)]
    pairs += [(value_hbm, value_v), (beta_hbm, beta_v), (up_hbm, up_v)]
    pairs += [
        (latq_hbm.at[:, pl.ds(h * rank, rank)], latq_v.at[pl.ds(h * TOK, TOK), :]) for h in range(heads)
    ]
    pairs += [(latent_hbm, keys.at[block_rows(SPAN, side)])]
    loads = [pltpu.make_async_copy(pairs[i][0], pairs[i][1], load_sem.at[i]) for i in range(len(pairs))]
    loads[0].start()
    loads[-1].start()
    for load in loads[1:-1]:
        load.start()

    barrier = pltpu.get_barrier_semaphore()

    def greet(peer):
        pl.semaphore_signal(barrier, inc=1, device_id=peer, device_id_type=MESH)

    for step in range(1, head_devices):
        greet((shard, lax.rem(side + step, head_devices)))
    for steps in (1,) + near:
        @pl.when(shard >= steps)
        def _(steps=steps):
            greet((ahead(-steps), side))

    @pl.when(is_a)
    def _():
        greet((ahead(1), side))

    def one_if(condition):
        return jnp.where(condition, 1, 0).astype(jnp.int32)

    expected = head_devices - 1 + core
    for steps in (1,) + near:
        expected = expected + one_if(shard + steps < shards)

    def near_copy(i):
        return pltpu.make_async_remote_copy(
            src_ref=latent_hbm, dst_ref=keys.at[block_rows(SPAN - near[i], side)],
            send_sem=near_send.at[i], recv_sem=near_recv.at[i],
            device_id=(ahead(near[i]), side), device_id_type=MESH,
        )

    def side_copy(i, step, place):
        rows = block_rows(SPAN - 2 * i, place)
        at = i * (head_devices - 1) + step - 1
        return pltpu.make_async_remote_copy(
            src_ref=keys.at[rows], dst_ref=keys.at[rows],
            send_sem=side_send.at[at], recv_sem=side_recv.at[at],
            device_id=(shard, lax.rem(side + step, head_devices)), device_id_type=MESH,
        )

    def side_start(i):
        for step in range(1, head_devices):
            side_copy(i, step, side).start()

    def side_arrived(i):
        for step in range(1, head_devices):
            side_copy(i, step, lax.rem(side + head_devices - step, head_devices)).wait_recv()

    def twin_copy(i):
        source = pl.ds(pl.multiple_of((2 * i + 2 * (1 - core)) * TOK, TOK), TOK)
        return pltpu.make_async_remote_copy(
            src_ref=keys.at[source], dst_ref=keys.at[pl.ds((2 * i + 1) * TOK, TOK)],
            send_sem=twin_send.at[i], recv_sem=twin_recv.at[i],
            device_id=(shard + 1 - 2 * core, side), device_id_type=MESH,
        )

    MAP_C, MAP_A, MAP_D, MAP_G, MAP_T = range(5)
    jump = {MAP_C: 1, MAP_A: -1, MAP_D: 1, MAP_G: 2, MAP_T: 1}

    def state_copy(kind, h):
        source = a_ref.at[h] if kind == MAP_A else send_buf.at[kind, h]
        return pltpu.make_async_remote_copy(
            src_ref=source, dst_ref=recv_buf.at[kind, h],
            send_sem=chain_send.at[kind, h], recv_sem=chain_recv.at[kind, h],
            device_id=(ahead(jump[kind]), side), device_id_type=MESH,
        )

    def send_state(kind, h, value=None):
        if value is not None:
            send_buf[kind, h] = value.astype(BF16)
        state_copy(kind, h).start()

    def take_state(kind, h):
        state_copy(kind, h).wait_recv()
        return recv_buf[kind, h]

    sends = {
        MAP_C: is_a,
        MAP_A: is_b,
        MAP_D: is_b & (chip < last),
        MAP_G: is_a & (chip > 0) & (chip < last),
        MAP_T: is_a,
    }
    span = range(heads)

    def emit(h, incoming):
        lanes = slice(h * WIDTH, (h + 1) * WIDTH)
        base[:, lanes] += mul(left_ref[h], incoming)

    loads[0].wait()
    prepare_masks(lens_v[...], shard, pair_mask, link_mask, level_mask, bias)
    pl.semaphore_wait(barrier, expected)
    for i in range(2):
        @pl.when(shard + near[i] < shards)
        def _(i=i):
            near_copy(i).start()
    loads[-1].wait()
    side_start(0)

    for load in loads[1:6]:
        load.wait()
    parts = delta_pairs(heads, (query_v, key_v, value_v, decay_v, beta_v), pair_mask, link_mask)

    for i in range(2):
        @pl.when(shard >= near[i])
        def _(i=i):
            near_copy(i).wait_recv()

        @pl.when(shard < near[i])
        def _(i=i):
            keys[block_rows(SPAN - near[i], side), :] = jnp.zeros((quarter, rank), BF16)

        side_start(i + 1)

    solved = delta_solve(parts, level_mask, a_ref, c_ref)

    @pl.when(is_a)
    def _():
        for h in span:
            send_state(MAP_C, h, c_ref[h])

    @pl.when(is_b)
    def _():
        for h in span:
            send_state(MAP_A, h)

    delta_outputs(parts, solved, left_ref, base)

    @pl.when(is_b)
    def _():
        for h in span:
            incoming = take_state(MAP_C, h)

            @pl.when(chip < last)
            def _():
                send_state(MAP_D, h, c_ref[h] + mul(a_ref[h], incoming))

    @pl.when(is_a)
    def _():
        for h in span:
            step_ref[h] = mul(take_state(MAP_A, h), a_ref[h]).astype(BF16)

    for i in range(SPAN // 2 + 1):
        side_arrived(i)
    for i in range(2):
        twin_copy(i).start()
    for load in loads[6:-1]:
        load.wait()
    for i in range(2):
        twin_copy(i).wait_recv()

    def latent_at(part):
        latent_part(part * 2, 2, scale, latq_v, keys, bias, up_v, mla_v)

    latent_at(0)
    latent_at(1)
    latent_at(2)

    @pl.when(is_a & (chip > 0))
    def _():
        for h in span:
            incoming = take_state(MAP_D, h)

            @pl.when(chip < last)
            def _():
                send_state(MAP_G, h, mul(step_ref[h], incoming))

        for h in span:
            c_ref[h] += mul(a_ref[h], recv_buf[MAP_D, h])
            emit(h, recv_buf[MAP_D, h])

    latent_at(3)

    @pl.when(is_a & (chip <= 1))
    def _():
        for h in span:
            send_state(MAP_T, h, c_ref[h])

    @pl.when(is_a & (chip > 1))
    def _():
        for h in span:
            incoming = take_state(MAP_G, h)
            send_state(MAP_T, h, c_ref[h] + mul(a_ref[h], incoming))
        for h in span:
            emit(h, recv_buf[MAP_G, h])

    @pl.when(is_b)
    def _():
        for h in span:
            emit(h, take_state(MAP_T, h))

    for i in range(2):
        @pl.when(shard + near[i] < shards)
        def _(i=i):
            near_copy(i).wait_send()

        twin_copy(i).wait_send()
    for i in range(SPAN // 2 + 1):
        for step in range(1, head_devices):
            side_copy(i, step, side).wait_send()
    for kind, condition in sends.items():
        @pl.when(condition)
        def _(kind=kind):
            for h in span:
                state_copy(kind, h).wait_send()


def solution(mesh):
    shards = mesh.shape["context"]
    head_devices = mesh.shape["head"]

    def step(query_vec, key_vec, value_vec, log_decay, beta, latent, latent_query, w_uv, doc_lengths):
        rows = query_vec.shape[0]
        heads = beta.shape[1]
        rank = w_uv.shape[0]
        width = query_vec.shape[1]
        keys = (SPAN + 1) * rows
        square = (rows, rows)
        outside = pl.BlockSpec(memory_space=pltpu.HBM)
        inside = pl.BlockSpec(memory_space=pltpu.VMEM)
        dma = pltpu.SemaphoreType.DMA
        side_copies = (SPAN // 2 + 1) * (head_devices - 1)
        return pl.pallas_call(
            functools.partial(body, shards, head_devices, heads, WIDTH**-0.5),
            out_shape=(
                jax.ShapeDtypeStruct((rows, width), F32),
                jax.ShapeDtypeStruct((rows, width), BF16),
            ),
            in_specs=[outside] * 9,
            out_specs=(inside, inside),
            scratch_shapes=[
                pltpu.VMEM((rows, width), F32),
                pltpu.VMEM((rows, width), F32),
                pltpu.VMEM((rows, width), F32),
                pltpu.VMEM((rows, width), F32),
                pltpu.VMEM((heads, rows), F32),
                pltpu.VMEM((rows * heads, rank), BF16),
                pltpu.VMEM((rank, width), BF16),
                pltpu.VMEM((keys, rank), BF16),
                pltpu.VMEM((1, doc_lengths.shape[0]), jnp.int32),
                pltpu.VMEM((2,) + square, F32),
                pltpu.VMEM((2,) + square, F32),
                pltpu.VMEM((LEVELS + 1,) + square, BF16),
                pltpu.VMEM((rows, keys), F32),
                pltpu.VMEM((heads,) + square, BF16),
                pltpu.VMEM((heads,) + square, F32),
                pltpu.VMEM((heads,) + square, BF16),
                pltpu.VMEM((heads,) + square, BF16),
                pltpu.VMEM((5, heads) + square, BF16),
                pltpu.VMEM((5, heads) + square, BF16),
                dma((8 + heads,)),
                dma((5, heads)),
                dma((5, heads)),
                dma((2,)),
                dma((2,)),
                dma((side_copies,)),
                dma((side_copies,)),
                dma((2,)),
                dma((2,)),
            ],
            compiler_params=pltpu.CompilerParams(
                collective_id=0, has_side_effects=True, vmem_limit_bytes=60 * 1024 * 1024
            ),
            cost_estimate=pl.CostEstimate(flops=3_000_000_000, bytes_accessed=6_000_000, transcendentals=1_000_000),
            name="packed_attention",
        )(
            query_vec, key_vec, value_vec, log_decay, beta.T, latent, latent_query, w_uv,
            doc_lengths.reshape(1, -1),
        )

    return jax.shard_map(
        step,
        mesh=mesh,
        in_specs=(
            P("context", "head"),
            P("context", "head"),
            P("context", "head"),
            P("context", "head"),
            P("context", "head"),
            P(("context", "head"), None),
            P("context", "head"),
            P(None, "head"),
            P(),
        ),
        out_specs=(P("context", "head"), P("context", "head")),
        check_vma=False,
    )
```

time: 41.6 us -> 34.5 us (0.83)
  the two profiles are of different devices: /device:TPU:1 before, /device:TPU:7 now
where the time goes in v2:
time: 34.5 us; the launch traced here: 34.4 us
  Pallas kernels  31.1 us (90%)
  local copies, waits for them, and re-layouts  2.63 us (8%)
  between operations  0.65 us (2%)
    pallas_call x1, Pallas kernels, step(): pl.pallas_call(functools.partial(body, shards, head_devices, heads, WIDTH...  31.1 us
    unnamed x4, local copies, waits for them, and re-layouts  2.63 us

profile of v2, /device:TPU:7, one launch (start us, length us, event | category | flops | bytes accessed | tf_op | source)
XLA Modules:
  0.0 34.4 jit_solution(17388835384418370984)
XLA Ops:
  0.6 31.1 %packed_attention.1 = (f32[128,1024]{1,0:T(8,128)}, bf16[128,1024]{1,0:T(8,128)(2,1)}) custom-call(f32[128,1024]{1,0:T(8,128)} %query_hbm.1, f32[128,1024]{1,0:T(8,128)} %key_hbm.1, f32[128,1024]{1,0:T(8,128)} %value_hbm.1, f32[128,1024]{1,0:T(8,128)} %decay_hbm.1, f32[8,128]{1,0:T(8,128)} %bitcast.2, bf16[32,512]{1,0:T(8,128)(2,1)} %latent_hbm.1, ...), custom_call_target="tpu_custom_call" | custom-call | flops 3000000000 | bytes 6000000 | tf_op jit(solution)/shard_map/packed_attention/pallas_call | solution.py:420
  31.8 0.0 copy-start
  31.8 1.9 %copy.13 = f32[128,1024]{1,0:T(8,128)} copy(f32[128,1024]{1,0:T(8,128)} %get-tuple-element.4) | data formatting | bytes 1048576
  33.7 0.0 copy-done
  33.7 0.7 %copy.14 = bf16[128,1024]{1,0:T(8,128)(2,1)} copy(bf16[128,1024]{1,0:T(8,128)(2,1)S(1)} %copy-done) | data formatting | bytes 524288
Async XLA Ops:
  31.8 1.9 %copy-start = (bf16[128,1024]{1,0:T(8,128)(2,1)S(1)}, bf16[128,1024]{1,0:T(8,128)(2,1)}, u32[]{:S(2)}) copy-start(bf16[128,1024]{1,0:T(8,128)(2,1)} %get-tuple-element.5) | copy-start | bytes 786436

commit v3 on v2

--- a/solution.py
+++ b/solution.py
@@ -16,6 +16,7 @@
 TOK = 128
 WIDTH = 128
 LEVELS = 7
+BATCH = 4
 
 
 def mul(left, right):
@@ -177,6 +178,7 @@
     rank = latq_v.shape[1]
     quarter = TOK // head_devices
     near = (2, 4)
+    batch = BATCH
 
     def ahead(steps):
         return lax.rem(shard + shards + steps, shards)
@@ -254,22 +256,27 @@
     MAP_C, MAP_A, MAP_D, MAP_G, MAP_T = range(5)
     jump = {MAP_C: 1, MAP_A: -1, MAP_D: 1, MAP_G: 2, MAP_T: 1}
 
-    def state_copy(kind, h):
-        source = a_ref.at[h] if kind == MAP_A else send_buf.at[kind, h]
+    def state_copy(kind, group):
+        part = pl.ds(group * batch, batch)
+        source = a_ref.at[part] if kind == MAP_A else send_buf.at[kind, part]
         return pltpu.make_async_remote_copy(
-            src_ref=source, dst_ref=recv_buf.at[kind, h],
-            send_sem=chain_send.at[kind, h], recv_sem=chain_recv.at[kind, h],
+            src_ref=source, dst_ref=recv_buf.at[kind, part],
+            send_sem=chain_send.at[kind, group], recv_sem=chain_recv.at[kind, group],
             device_id=(ahead(jump[kind]), side), device_id_type=MESH,
         )
 
-    def send_state(kind, h, value=None):
-        if value is not None:
-            send_buf[kind, h] = value.astype(BF16)
-        state_copy(kind, h).start()
-
-    def take_state(kind, h):
-        state_copy(kind, h).wait_recv()
-        return recv_buf[kind, h]
+    def members(group):
+        return range(group * batch, (group + 1) * batch)
+
+    def send_state(kind, group, values=None):
+        if values is not None:
+            for h, value in zip(members(group), values):
+                send_buf[kind, h] = value.astype(BF16)
+        state_copy(kind, group).start()
+
+    def take_state(kind, group):
+        state_copy(kind, group).wait_recv()
+        return [recv_buf[kind, h] for h in members(group)]
 
     sends = {
         MAP_C: is_a,
@@ -278,11 +285,12 @@
         MAP_G: is_a & (chip > 0) & (chip < last),
         MAP_T: is_a,
     }
-    span = range(heads)
-
-    def emit(h, incoming):
-        lanes = slice(h * WIDTH, (h + 1) * WIDTH)
-        base[:, lanes] += mul(left_ref[h], incoming)
+    groups = range(heads // batch)
+
+    def emit(group, incoming):
+        for h, state in zip(members(group), incoming):
+            lanes = slice(h * WIDTH, (h + 1) * WIDTH)
+            base[:, lanes] += mul(left_ref[h], state)
 
     loads[0].wait()
     prepare_masks(lens_v[...], shard, pair_mask, link_mask, level_mask, bias)
@@ -298,6 +306,18 @@
         load.wait()
     parts = delta_pairs(heads, (query_v, key_v, value_v, decay_v, beta_v), pair_mask, link_mask)
 
+    solved = delta_solve(parts, level_mask, a_ref, c_ref)
+
+    @pl.when(is_a)
+    def _():
+        for group in groups:
+            send_state(MAP_C, group, [c_ref[h] for h in members(group)])
+
+    @pl.when(is_b)
+    def _():
+        for group in groups:
+            send_state(MAP_A, group)
+
     for i in range(2):
         @pl.when(shard >= near[i])
         def _(i=i):
@@ -309,82 +329,82 @@
 
         side_start(i + 1)
 
-    solved = delta_solve(parts, level_mask, a_ref, c_ref)
+    delta_outputs(parts, solved, left_ref, base)
+
+    @pl.when(is_b & (chip < last))
+    def _():
+        for group in groups:
+            incoming = take_state(MAP_C, group)
+            send_state(
+                MAP_D, group, [c_ref[h] + mul(a_ref[h], x) for h, x in zip(members(group), incoming)]
+            )
+
+    @pl.when(is_b & (chip == last))
+    def _():
+        for group in groups:
+            take_state(MAP_C, group)
 
     @pl.when(is_a)
     def _():
-        for h in span:
-            send_state(MAP_C, h, c_ref[h])
-
-    @pl.when(is_b)
-    def _():
-        for h in span:
-            send_state(MAP_A, h)
-
-    delta_outputs(parts, solved, left_ref, base)
-
-    @pl.when(is_b)
-    def _():
-        for h in span:
-            incoming = take_state(MAP_C, h)
-
-            @pl.when(chip < last)
-            def _():
-                send_state(MAP_D, h, c_ref[h] + mul(a_ref[h], incoming))
-
-    @pl.when(is_a)
-    def _():
-        for h in span:
-            step_ref[h] = mul(take_state(MAP_A, h), a_ref[h]).astype(BF16)
+        for group in groups:
+            incoming = take_state(MAP_A, group)
+            for h, x in zip(members(group), incoming):
+                step_ref[h] = mul(x, a_ref[h]).astype(BF16)
 
     for i in range(SPAN // 2 + 1):
         side_arrived(i)
     for i in range(2):
         twin_copy(i).start()
+
+    @pl.when(is_a & (chip > 0) & (chip < last))
+    def _():
+        for group in groups:
+            incoming = take_state(MAP_D, group)
+            send_state(MAP_G, group, [mul(step_ref[h], x) for h, x in zip(members(group), incoming)])
+
+    @pl.when(is_a & (chip == last))
+    def _():
+        for group in groups:
+            take_state(MAP_D, group)
+
     for load in loads[6:-1]:
         load.wait()
     for i in range(2):
         twin_copy(i).wait_recv()
 
     def latent_at(part):
-        latent_part(part * 2, 2, scale, latq_v, keys, bias, up_v, mla_v)
+        latent_part(part * 4, 4, scale, latq_v, keys, bias, up_v, mla_v)
 
     latent_at(0)
+
     latent_at(1)
-    latent_at(2)
 
     @pl.when(is_a & (chip > 0))
     def _():
-        for h in span:
-            incoming = take_state(MAP_D, h)
-
-            @pl.when(chip < last)
-            def _():
-                send_state(MAP_G, h, mul(step_ref[h], incoming))
-
-        for h in span:
-            c_ref[h] += mul(a_ref[h], recv_buf[MAP_D, h])
-            emit(h, recv_buf[MAP_D, h])
-
-    latent_at(3)
+        for group in groups:
+            for h in members(group):
+                c_ref[h] += mul(a_ref[h], recv_buf[MAP_D, h])
+            emit(group, [recv_buf[MAP_D, h] for h in members(group)])
 
     @pl.when(is_a & (chip <= 1))
     def _():
-        for h in span:
-            send_state(MAP_T, h, c_ref[h])
+        for group in groups:
+            send_state(MAP_T, group, [c_ref[h] for h in members(group)])
 
     @pl.when(is_a & (chip > 1))
     def _():
-        for h in span:
-            incoming = take_state(MAP_G, h)
-            send_state(MAP_T, h, c_ref[h] + mul(a_ref[h], incoming))
-        for h in span:
-            emit(h, recv_buf[MAP_G, h])
+        for group in groups:
+            incoming = take_state(MAP_G, group)
+            send_state(
+                MAP_T, group, [c_ref[h] + mul(a_ref[h], x) for h, x in zip(members(group), incoming)]
+            )
+        for group in groups:
+            emit(group, [recv_buf[MAP_G, h] for h in members(group)])
 
     @pl.when(is_b)
     def _():
-        for h in span:
-            emit(h, take_state(MAP_T, h))
+        for group in groups:
+            emit(group, take_state(MAP_T, group))
 
     for i in range(2):
         @pl.when(shard + near[i] < shards)
@@ -398,8 +418,8 @@
     for kind, condition in sends.items():
         @pl.when(condition)
         def _(kind=kind):
-            for h in span:
-                state_copy(kind, h).wait_send()
+            for group in groups:
+                state_copy(kind, group).wait_send()
 
 
 def solution(mesh):
@@ -417,6 +437,8 @@
         inside = pl.BlockSpec(memory_space=pltpu.VMEM)
         dma = pltpu.SemaphoreType.DMA
         side_copies = (SPAN // 2 + 1) * (head_devices - 1)
+        inputs = (query_vec, key_vec, value_vec, log_decay, beta.T, latent, latent_query, w_uv, doc_lengths.reshape(1, -1))
+        inputs = [pltpu.with_memory_space_constraint(x, pltpu.HBM) for x in inputs]
         return pl.pallas_call(
             functools.partial(body, shards, head_devices, heads, WIDTH**-0.5),
             out_shape=(
@@ -446,8 +468,8 @@
                 pltpu.VMEM((5, heads) + square, BF16),
                 pltpu.VMEM((5, heads) + square, BF16),
                 dma((8 + heads,)),
-                dma((5, heads)),
-                dma((5, heads)),
+                dma((5, heads // BATCH)),
+                dma((5, heads // BATCH)),
                 dma((2,)),
                 dma((2,)),
                 dma((side_copies,)),
@@ -456,14 +478,11 @@
                 dma((2,)),
             ],
             compiler_params=pltpu.CompilerParams(
-                collective_id=0, has_side_effects=True, vmem_limit_bytes=60 * 1024 * 1024
+                collective_id=0, has_side_effects=True, vmem_limit_bytes=48 * 1024 * 1024
             ),
             cost_estimate=pl.CostEstimate(flops=3_000_000_000, bytes_accessed=6_000_000, transcendentals=1_000_000),
             name="packed_attention",
-        )(
-            query_vec, key_vec, value_vec, log_decay, beta.T, latent, latent_query, w_uv,
-            doc_lengths.reshape(1, -1),
-        )
+        )(*inputs)
 
     return jax.shard_map(
         step,

time: 34.5 us -> 28 us (0.81)
  Pallas kernels: 31.1 us -> 25.8 us
  local copies, waits for them, and re-layouts: 2.63 us -> 1.5 us
    pallas_call x1, Pallas kernels: 31.1 us -> 25.8 us  [step(): pl.pallas_call(functools.partial(body, shards, head_devices, heads, WIDTH...]
    unnamed x4 -> x2, local copies, waits for them, and re-layouts: 2.63 us -> 1.5 us
where the time goes in v3:
time: 28 us
  Pallas kernels  25.8 us (92%)
  local copies, waits for them, and re-layouts  1.5 us (5%)
  between operations  0.64 us (2%)
    pallas_call x1, Pallas kernels, step(): pl.pallas_call(functools.partial(body, shards, head_devices, heads, WIDTH...  25.8 us
    unnamed x2, local copies, waits for them, and re-layouts  1.5 us

profile of v3, /device:TPU:7, one launch (start us, length us, event | category | flops | bytes accessed | tf_op | source)
XLA Modules:
  0.0 28.0 jit_solution(3115727324320515962)
XLA Ops:
  0.6 25.8 %packed_attention.1 = (f32[128,1024]{1,0:T(8,128)S(1)}, bf16[128,1024]{1,0:T(8,128)(2,1)S(1)}) custom-call(f32[128,1024]{1,0:T(8,128)} %query_hbm.1, f32[128,1024]{1,0:T(8,128)} %key_hbm.1, f32[128,1024]{1,0:T(8,128)} %value_hbm.1, f32[128,1024]{1,0:T(8,128)} %decay_hbm.1, f32[8,128]{1,0:T(8,128)} %bitcast.2, bf16[32,512]{1,0:T(8,128)(2,1)} %latent_hbm.1, ...), custom_call_target="tpu_custom_call" | custom-call | flops 3000000000 | bytes 6000000 | tf_op jit(solution)/shard_map/packed_attention/pallas_call | solution.py:442
  26.5 0.8 %copy.13 = f32[128,1024]{1,0:T(8,128)} copy(f32[128,1024]{1,0:T(8,128)S(1)} %get-tuple-element.4) | data formatting | bytes 1048576
  27.2 0.7 %copy.14 = bf16[128,1024]{1,0:T(8,128)(2,1)} copy(bf16[128,1024]{1,0:T(8,128)(2,1)S(1)} %get-tuple-element.5) | data formatting | bytes 524288

commit v4 on v3

--- a/solution.py
+++ b/solution.py
@@ -116,7 +116,7 @@
     return parts
 
 
-def delta_solve(parts, level_mask, a_ref, c_ref):
+def delta_solve(parts, level_mask, a_ref, c_ref, midway, finished):
     square = (TOK, TOK)
     row, col = iota2(square, 0), iota2(square, 1)
     system = [part["system"] for part in parts]
@@ -124,15 +124,19 @@
     span = range(len(parts))
     inverse = [level_mask[LEVELS] - system[h][0] * level_mask[0] for h in span]
     for level in range(1, LEVELS):
+        if level == LEVELS // 2:
+            midway()
         inner = [mul(system[h][0] * level_mask[level], inverse[h]).astype(BF16) for h in span]
         inverse = [inverse[h] - mul(inverse[h], inner[h]).astype(BF16) for h in span]
     solved = [mul(inverse[h], right[h].astype(BF16)) for h in span]
     rest = [right[h] - solved[h] - three(mul, system[h], halves(solved[h])) for h in span]
     solved = [halves(solved[h] + mul(inverse[h], rest[h].astype(BF16))) for h in span]
-    for h in span:
-        change = three(mul_tn, parts[h]["tail"], solved[h])
-        c_ref[h] = change[:, :WIDTH]
-        a_ref[h] = (jnp.where(row == col, parts[h]["end"], 0.0) - change[:, WIDTH:]).astype(BF16)
+    for group in range(len(parts) // BATCH):
+        for h in range(group * BATCH, (group + 1) * BATCH):
+            change = three(mul_tn, parts[h]["tail"], solved[h])
+            c_ref[h] = change[:, :WIDTH]
+            a_ref[h] = (jnp.where(row == col, parts[h]["end"], 0.0) - change[:, WIDTH:]).astype(BF16)
+        finished(group)
     return solved
 
 
@@ -294,29 +298,51 @@
 
     loads[0].wait()
     prepare_masks(lens_v[...], shard, pair_mask, link_mask, level_mask, bias)
-    pl.semaphore_wait(barrier, expected)
-    for i in range(2):
-        @pl.when(shard + near[i] < shards)
-        def _(i=i):
-            near_copy(i).start()
-    loads[-1].wait()
-    side_start(0)
-
     for load in loads[1:6]:
         load.wait()
     parts = delta_pairs(heads, (query_v, key_v, value_v, decay_v, beta_v), pair_mask, link_mask)
 
-    solved = delta_solve(parts, level_mask, a_ref, c_ref)
+    def open_links():
+        pl.semaphore_wait(barrier, expected)
+        for i in range(2):
+            @pl.when(shard + near[i] < shards)
+            def _(i=i):
+                near_copy(i).start()
+        loads[-1].wait()
+        side_start(0)
+
+    def send_maps(group):
+        @pl.when(is_a)
+        def _():
+            send_state(MAP_C, group, [c_ref[h] for h in members(group)])
+
+        @pl.when(is_b)
+        def _():
+            send_state(MAP_A, group)
+
+    solved = delta_solve(parts, level_mask, a_ref, c_ref, open_links, send_maps)
+
+    delta_outputs(parts, solved, left_ref, base)
+
+    @pl.when(is_b & (chip < last))
+    def _():
+        for group in groups:
+            incoming = take_state(MAP_C, group)
+            send_state(
+                MAP_D, group, [c_ref[h] + mul(a_ref[h], x) for h, x in zip(members(group), incoming)]
+            )
+
+    @pl.when(is_b & (chip == last))
+    def _():
+        for group in groups:
+            take_state(MAP_C, group)
 
     @pl.when(is_a)
     def _():
         for group in groups:
-            send_state(MAP_C, group, [c_ref[h] for h in members(group)])
-
-    @pl.when(is_b)
-    def _():
-        for group in groups:
-            send_state(MAP_A, group)
+            incoming = take_state(MAP_A, group)
+            for h, x in zip(members(group), incoming):
+                step_ref[h] = mul(x, a_ref[h]).astype(BF16)
 
     for i in range(2):
         @pl.when(shard >= near[i])
@@ -329,33 +355,6 @@
 
         side_start(i + 1)
 
-    delta_outputs(parts, solved, left_ref, base)
-
-    @pl.when(is_b & (chip < last))
-    def _():
-        for group in groups:
-            incoming = take_state(MAP_C, group)
-            send_state(
-                MAP_D, group, [c_ref[h] + mul(a_ref[h], x) for h, x in zip(members(group), incoming)]
-            )
-
-    @pl.when(is_b & (chip == last))
-    def _():
-        for group in groups:
-            take_state(MAP_C, group)
-
-    @pl.when(is_a)
-    def _():
-        for group in groups:
-            incoming = take_state(MAP_A, group)
-            for h, x in zip(members(group), incoming):
-                step_ref[h] = mul(x, a_ref[h]).astype(BF16)
-
-    for i in range(SPAN // 2 + 1):
-        side_arrived(i)
-    for i in range(2):
-        twin_copy(i).start()
-
     @pl.when(is_a & (chip > 0) & (chip < last))
     def _():
         for group in groups:
@@ -366,6 +365,28 @@
     def _():
         for group in groups:
             take_state(MAP_D, group)
+
+    side_arrived(0)
+
+    @pl.when(is_a)
+    def _():
+        twin_copy(1).start()
+
+    side_arrived(1)
+
+    @pl.when(is_a)
+    def _():
+        twin_copy(0).start()
+
+    @pl.when(is_b)
+    def _():
+        twin_copy(1).start()
+
+    side_arrived(2)
+
+    @pl.when(is_b)
+    def _():
+        twin_copy(0).start()
 
     for load in loads[6:-1]:
         load.wait()
@@ -377,29 +398,40 @@
 
     latent_at(0)
 
-    latent_at(1)
-
-    @pl.when(is_a & (chip > 0))
-    def _():
-        for group in groups:
-            for h in members(group):
-                c_ref[h] += mul(a_ref[h], recv_buf[MAP_D, h])
-            emit(group, [recv_buf[MAP_D, h] for h in members(group)])
-
     @pl.when(is_a & (chip <= 1))
     def _():
+        @pl.when(chip == 1)
+        def _():
+            for group in groups:
+                for h in members(group):
+                    c_ref[h] += mul(a_ref[h], recv_buf[MAP_D, h])
+
         for group in groups:
             send_state(MAP_T, group, [c_ref[h] for h in members(group)])
 
     @pl.when(is_a & (chip > 1))
     def _():
+        for h in range(heads):
+            c_ref[h] += mul(a_ref[h], recv_buf[MAP_D, h])
         for group in groups:
             incoming = take_state(MAP_G, group)
             send_state(
                 MAP_T, group, [c_ref[h] + mul(a_ref[h], x) for h, x in zip(members(group), incoming)]
             )
-        for group in groups:
-            emit(group, [recv_buf[MAP_G, h] for h in members(group)])
+
+    latent_at(1)
+
+    @pl.when(is_a & (chip == 1))
+    def _():
+        for group in groups:
+            emit(group, [recv_buf[MAP_D, h] for h in members(group)])
+
+    @pl.when(is_a & (chip > 1))
+    def _():
+        for group in groups:
+            for h in members(group):
+                lanes = slice(h * WIDTH, (h + 1) * WIDTH)
+                base[:, lanes] += mul(left_ref[h], recv_buf[MAP_D, h]) + mul(left_ref[h], recv_buf[MAP_G, h])
 
     @pl.when(is_b)
     def _():

time: 28 us -> 26.4 us (0.943); the launches traced: 28 us -> 26.1 us
  Pallas kernels: 25.8 us -> 23.9 us
    pallas_call x1, Pallas kernels: 25.8 us -> 23.9 us  [step(): pl.pallas_call(functools.partial(body, shards, head_devices, heads, WIDTH...]
where the time goes in v4:
time: 26.4 us; the launch traced here: 26.1 us
  Pallas kernels  23.9 us (91%)
  local copies, waits for them, and re-layouts  1.5 us (6%)
  between operations  0.64 us (2%)
    pallas_call x1, Pallas kernels, step(): pl.pallas_call(functools.partial(body, shards, head_devices, heads, WIDTH...  23.9 us
    unnamed x2, local copies, waits for them, and re-layouts  1.5 us

profile of v4, /device:TPU:7, one launch (start us, length us, event | category | flops | bytes accessed | tf_op | source)
XLA Modules:
  0.0 26.1 jit_solution(9825398243877804919)
XLA Ops:
  0.6 23.9 %packed_attention.1 = (f32[128,1024]{1,0:T(8,128)S(1)}, bf16[128,1024]{1,0:T(8,128)(2,1)S(1)}) custom-call(f32[128,1024]{1,0:T(8,128)} %query_hbm.1, f32[128,1024]{1,0:T(8,128)} %key_hbm.1, f32[128,1024]{1,0:T(8,128)} %value_hbm.1, f32[128,1024]{1,0:T(8,128)} %decay_hbm.1, f32[8,128]{1,0:T(8,128)} %bitcast.2, bf16[32,512]{1,0:T(8,128)(2,1)} %latent_hbm.1, ...), custom_call_target="tpu_custom_call" | custom-call | flops 3000000000 | bytes 6000000 | tf_op jit(solution)/shard_map/packed_attention/pallas_call | solution.py:474
  24.6 0.8 %copy.13 = f32[128,1024]{1,0:T(8,128)} copy(f32[128,1024]{1,0:T(8,128)S(1)} %get-tuple-element.4) | data formatting | bytes 1048576
  25.4 0.7 %copy.14 = bf16[128,1024]{1,0:T(8,128)(2,1)} copy(bf16[128,1024]{1,0:T(8,128)(2,1)S(1)} %get-tuple-element.5) | data formatting | bytes 524288

commit v5 on v4

--- a/solution.py
+++ b/solution.py
@@ -17,6 +17,7 @@
 WIDTH = 128
 LEVELS = 7
 BATCH = 4
+PIECES = 2
 
 
 def mul(left, right):
@@ -44,7 +45,7 @@
     return lax.broadcasted_iota(jnp.int32, shape, axis)
 
 
-def prepare_masks(lens, shard, pair_mask, link_mask, level_mask, bias):
+def prepare_masks(lens, shard, pair_mask, link_mask, level_mask):
     square = (TOK, TOK)
     row, col = iota2(square, 0), iota2(square, 1)
     lens_f = lens.astype(F32)
@@ -55,12 +56,9 @@
     low = shard * TOK
     pos_col = (low + iota2((TOK, 1), 0)).astype(F32)
     start_col = jnp.max(jnp.where(begin_row <= pos_col, begin_row, -1.0), axis=1, keepdims=True)
-    keys = (SPAN + 1) * TOK
-    pos_row = (low - SPAN * TOK + iota2((1, keys), 1)).astype(F32)
+    pos_row = (low + iota2((1, TOK), 1)).astype(F32)
     start_row = jnp.max(jnp.where(begin_col <= pos_row, begin_col, -1.0), axis=0, keepdims=True)
-    visible = (start_col == start_row) & (pos_row <= pos_col)
-    bias[...] = jnp.where(visible, 0.0, FAR)
-    same = start_col == start_row[:, SPAN * TOK :]
+    same = start_col == start_row
     pair_mask[0] = jnp.where(same & (row >= col), 1.0, 0.0)
     pair_mask[1] = jnp.where(same & (row > col), 1.0, 0.0)
     link_mask[0] = jnp.broadcast_to(jnp.where(start_col < low.astype(F32), 1.0, 0.0), square)
@@ -69,14 +67,24 @@
         below = ((row >> (level + 1)) == (col >> (level + 1))) & ((row >> level) > (col >> level))
         level_mask[level] = jnp.where(below, 1.0, 0.0).astype(BF16)
     level_mask[LEVELS] = jnp.where(row == col, 1.0, 0.0).astype(BF16)
+    return begin_col, start_col, pos_col
+
+
+def prepare_bias(found, shard, bias):
+    begin_col, start_col, pos_col = found
+    keys = (SPAN + 1) * TOK
+    pos_row = ((shard - SPAN) * TOK + iota2((1, keys), 1)).astype(F32)
+    start_row = jnp.max(jnp.where(begin_col <= pos_row, begin_col, -1.0), axis=0, keepdims=True)
+    visible = (start_col == start_row) & (pos_row <= pos_col)
+    bias[...] = jnp.where(visible, 0.0, FAR)
 
 
 def delta_pairs(heads, refs, pair_mask, link_mask):
-    query_ref, key_ref, value_ref, decay_ref, beta_ref = refs
+    key_ref, value_ref, decay_ref, beta_ref = refs
     square = (TOK, TOK)
     row, col = iota2(square, 0), iota2(square, 1)
     lower = jnp.where(row >= col, 1.0, 0.0).astype(BF16)
-    incl, strict = pair_mask[0] > 0.5, pair_mask[1] > 0.5
+    strict = pair_mask[1] > 0.5
     link, tail = link_mask[0], link_mask[1]
     link_last = link[TOK - 1 :, :]
     beta_cols = beta_ref[...].T
@@ -92,20 +100,19 @@
         centre, end = cum[TOK // 2 - 1 : TOK // 2, :], cum[TOK - 1 :, :]
         grow, shrink = jnp.exp(cum - centre), jnp.exp(centre - cum)
         from_start, to_end = jnp.exp(centre), jnp.exp(end - centre)
-        query, key = query_ref[:, lanes], key_ref[:, lanes]
-        query = query * lax.rsqrt(jnp.sum(query * query, axis=1, keepdims=True) + EPS)
+        key = key_ref[:, lanes]
         key = key * lax.rsqrt(jnp.sum(key * key, axis=1, keepdims=True) + EPS)
-        query_grow, key_grow, key_shrink = query * grow, key * grow, key * shrink
-        pairs = three(
-            mul_nt, halves(jnp.concatenate([query_grow, key_grow], axis=0)), halves(key_shrink)
-        )
+        key_grow, key_shrink = key * grow, key * shrink
+        shrunk = halves(key_shrink)
+        pairs = three(mul_nt, halves(key_grow), shrunk)
         beta = beta_cols[:, h : h + 1]
         in_scale = link * from_start
         parts.append(
             dict(
-                weight=halves(jnp.where(incl, pairs[:TOK], 0.0)),
-                system=halves(jnp.where(strict, pairs[TOK:], 0.0) * beta),
-                query_in=query_grow * in_scale,
+                grow=grow,
+                shrunk=shrunk,
+                in_scale=in_scale,
+                system=halves(jnp.where(strict, pairs, 0.0) * beta),
                 right=jnp.concatenate(
                     [value_ref[:, lanes] * beta, key_grow * in_scale * beta], axis=1
                 ),
@@ -124,7 +131,7 @@
     span = range(len(parts))
     inverse = [level_mask[LEVELS] - system[h][0] * level_mask[0] for h in span]
     for level in range(1, LEVELS):
-        if level == LEVELS // 2:
+        if level == 1:
             midway()
         inner = [mul(system[h][0] * level_mask[level], inverse[h]).astype(BF16) for h in span]
         inverse = [inverse[h] - mul(inverse[h], inner[h]).astype(BF16) for h in span]
@@ -140,11 +147,17 @@
     return solved
 
 
-def delta_outputs(parts, solved, left_ref, base_ref):
-    for h in range(len(parts)):
-        output = three(mul, parts[h]["weight"], solved[h])
-        base_ref[:, h * WIDTH : (h + 1) * WIDTH] = output[:, :WIDTH]
-        left_ref[h] = (parts[h]["query_in"] - output[:, WIDTH:]).astype(BF16)
+def delta_outputs(parts, solved, query_ref, pair_mask, left_ref, base_ref):
+    incl = pair_mask[0] > 0.5
+    for h, part in enumerate(parts):
+        lanes = slice(h * WIDTH, (h + 1) * WIDTH)
+        query = query_ref[:, lanes]
+        query = query * lax.rsqrt(jnp.sum(query * query, axis=1, keepdims=True) + EPS)
+        query = query * part["grow"]
+        weight = jnp.where(incl, three(mul_nt, halves(query), part["shrunk"]), 0.0)
+        output = three(mul, halves(weight), solved[h])
+        base_ref[:, lanes] = output[:, :WIDTH]
+        left_ref[h] = (query * part["in_scale"] - output[:, WIDTH:]).astype(BF16)
 
 
 def latent_part(first, heads, scale, query_rows, keys, bias, up_ref, out_ref):
@@ -190,8 +203,8 @@
     def block_rows(block, place):
         return pl.ds(pl.multiple_of(block * TOK + place * quarter, quarter), quarter)
 
-    pairs = [(lens_hbm, lens_v), (decay_hbm, decay_v), (key_hbm, key_v), (query_hbm, query_v)]
-    pairs += [(value_hbm, value_v), (beta_hbm, beta_v), (up_hbm, up_v)]
+    pairs = [(lens_hbm, lens_v), (decay_hbm, decay_v), (key_hbm, key_v), (beta_hbm, beta_v)]
+    pairs += [(value_hbm, value_v), (query_hbm, query_v), (up_hbm, up_v)]
     pairs += [
         (latq_hbm.at[:, pl.ds(h * rank, rank)], latq_v.at[pl.ds(h * TOK, TOK), :]) for h in range(heads)
     ]
@@ -209,20 +222,17 @@
 
     for step in range(1, head_devices):
         greet((shard, lax.rem(side + step, head_devices)))
-    for steps in (1,) + near:
+    greet((shard + 1 - 2 * core, side))
+    for steps in near:
         @pl.when(shard >= steps)
         def _(steps=steps):
             greet((ahead(-steps), side))
 
-    @pl.when(is_a)
-    def _():
-        greet((ahead(1), side))
-
     def one_if(condition):
         return jnp.where(condition, 1, 0).astype(jnp.int32)
 
-    expected = head_devices - 1 + core
-    for steps in (1,) + near:
+    expected = head_devices
+    for steps in near:
         expected = expected + one_if(shard + steps < shards)
 
     def near_copy(i):
@@ -257,12 +267,17 @@
             device_id=(shard + 1 - 2 * core, side), device_id_type=MESH,
         )
 
-    MAP_C, MAP_A, MAP_D, MAP_G, MAP_T = range(5)
-    jump = {MAP_C: 1, MAP_A: -1, MAP_D: 1, MAP_G: 2, MAP_T: 1}
+    MAP_C, MAP_A, MAP_D, MAP_G, MAP_X, MAP_Y = range(6)
+    jump = {MAP_C: 1, MAP_A: 1, MAP_D: 2, MAP_G: 2, MAP_X: -1, MAP_Y: -1}
 
     def state_copy(kind, group):
         part = pl.ds(group * batch, batch)
-        source = a_ref.at[part] if kind == MAP_A else send_buf.at[kind, part]
+        if kind == MAP_A:
+            source = a_ref.at[part]
+        elif kind in (MAP_X, MAP_Y):
+            source = recv_buf.at[MAP_D if kind == MAP_X else MAP_G, part]
+        else:
+            source = send_buf.at[kind, part]
         return pltpu.make_async_remote_copy(
             src_ref=source, dst_ref=recv_buf.at[kind, part],
             send_sem=chain_send.at[kind, group], recv_sem=chain_recv.at[kind, group],
@@ -284,10 +299,11 @@
 
     sends = {
         MAP_C: is_a,
-        MAP_A: is_b,
+        MAP_A: is_a,
         MAP_D: is_b & (chip < last),
-        MAP_G: is_a & (chip > 0) & (chip < last),
-        MAP_T: is_a,
+        MAP_G: is_b & (chip > 0) & (chip < last),
+        MAP_X: is_b & (chip > 0),
+        MAP_Y: is_b & (chip > 1),
     }
     groups = range(heads // batch)
 
@@ -297,10 +313,10 @@
             base[:, lanes] += mul(left_ref[h], state)
 
     loads[0].wait()
-    prepare_masks(lens_v[...], shard, pair_mask, link_mask, level_mask, bias)
-    for load in loads[1:6]:
+    found = prepare_masks(lens_v[...], shard, pair_mask, link_mask, level_mask)
+    for load in loads[1:5]:
         load.wait()
-    parts = delta_pairs(heads, (query_v, key_v, value_v, decay_v, beta_v), pair_mask, link_mask)
+    parts = delta_pairs(heads, (key_v, value_v, decay_v, beta_v), pair_mask, link_mask)
 
     def open_links():
         pl.semaphore_wait(barrier, expected)
@@ -316,13 +332,15 @@
         def _():
             send_state(MAP_C, group, [c_ref[h] for h in members(group)])
 
-        @pl.when(is_b)
-        def _():
+    solved = delta_solve(parts, level_mask, a_ref, c_ref, open_links, send_maps)
+
+    @pl.when(is_a)
+    def _():
+        for group in groups:
             send_state(MAP_A, group)
 
-    solved = delta_solve(parts, level_mask, a_ref, c_ref, open_links, send_maps)
-
-    delta_outputs(parts, solved, left_ref, base)
+    loads[5].wait()
+    delta_outputs(parts, solved, query_v, pair_mask, left_ref, base)
 
     @pl.when(is_b & (chip < last))
     def _():
@@ -337,12 +355,12 @@
         for group in groups:
             take_state(MAP_C, group)
 
-    @pl.when(is_a)
+    @pl.when(is_b)
     def _():
         for group in groups:
             incoming = take_state(MAP_A, group)
             for h, x in zip(members(group), incoming):
-                step_ref[h] = mul(x, a_ref[h]).astype(BF16)
+                step_ref[h] = mul(a_ref[h], x).astype(BF16)
 
     for i in range(2):
         @pl.when(shard >= near[i])
@@ -355,16 +373,20 @@
 
         side_start(i + 1)
 
-    @pl.when(is_a & (chip > 0) & (chip < last))
+    @pl.when(is_b & (chip > 0) & (chip < last))
     def _():
         for group in groups:
             incoming = take_state(MAP_D, group)
             send_state(MAP_G, group, [mul(step_ref[h], x) for h, x in zip(members(group), incoming)])
-
-    @pl.when(is_a & (chip == last))
+            send_state(MAP_X, group)
+
+    @pl.when(is_b & (chip == last))
     def _():
         for group in groups:
             take_state(MAP_D, group)
+            send_state(MAP_X, group)
+
+    prepare_bias(found, shard, bias)
 
     side_arrived(0)
 
@@ -398,45 +420,57 @@
 
     latent_at(0)
 
-    @pl.when(is_a & (chip <= 1))
-    def _():
-        @pl.when(chip == 1)
-        def _():
-            for group in groups:
-                for h in members(group):
-                    c_ref[h] += mul(a_ref[h], recv_buf[MAP_D, h])
-
-        for group in groups:
-            send_state(MAP_T, group, [c_ref[h] for h in members(group)])
+    @pl.when(is_b & (chip > 1))
+    def _():
+        for group in groups:
+            take_state(MAP_G, group)
+            send_state(MAP_Y, group)
+
+    latent_at(1)
+
+    def start_of(h):
+        return recv_buf[MAP_C, h].astype(F32)
+
+    def add_out(group, incoming):
+        for h, state in zip(members(group), incoming):
+            lanes = slice(h * WIDTH, (h + 1) * WIDTH)
+            base[:, lanes] += mul(left_ref[h], state.astype(BF16))
+
+    @pl.when(is_b & (chip == 0))
+    def _():
+        for group in groups:
+            add_out(group, [recv_buf[MAP_C, h] for h in members(group)])
+
+    @pl.when(is_b & (chip == 1))
+    def _():
+        for group in groups:
+            add_out(
+                group,
+                [start_of(h) + mul(recv_buf[MAP_A, h], recv_buf[MAP_D, h]) for h in members(group)],
+            )
+
+    @pl.when(is_b & (chip > 1))
+    def _():
+        for group in groups:
+            add_out(
+                group,
+                [
+                    start_of(h)
+                    + mul(recv_buf[MAP_A, h], recv_buf[MAP_D, h])
+                    + mul(recv_buf[MAP_A, h], recv_buf[MAP_G, h])
+                    for h in members(group)
+                ],
+            )
+
+    @pl.when(is_a & (chip > 0))
+    def _():
+        for group in groups:
+            emit(group, take_state(MAP_X, group))
 
     @pl.when(is_a & (chip > 1))
     def _():
-        for h in range(heads):
-            c_ref[h] += mul(a_ref[h], recv_buf[MAP_D, h])
-        for group in groups:
-            incoming = take_state(MAP_G, group)
-            send_state(
-                MAP_T, group, [c_ref[h] + mul(a_ref[h], x) for h, x in zip(members(group), incoming)]
-            )
-
-    latent_at(1)
-
-    @pl.when(is_a & (chip == 1))
-    def _():
-        for group in groups:
-            emit(group, [recv_buf[MAP_D, h] for h in members(group)])
-
-    @pl.when(is_a & (chip > 1))
-    def _():
-        for group in groups:
-            for h in members(group):
-                lanes = slice(h * WIDTH, (h + 1) * WIDTH)
-                base[:, lanes] += mul(left_ref[h], recv_buf[MAP_D, h]) + mul(left_ref[h], recv_buf[MAP_G, h])
-
-    @pl.when(is_b)
-    def _():
-        for group in groups:
-            emit(group, take_state(MAP_T, group))
+        for group in groups:
+            emit(group, take_state(MAP_Y, group))
 
     for i in range(2):
         @pl.when(shard + near[i] < shards)
@@ -452,6 +486,21 @@
         def _(kind=kind):
             for group in groups:
                 state_copy(kind, group).wait_send()
+
+
+def write_out(delta_ref, mla_ref, delta_hbm, mla_hbm, sem):
+    copies = []
+    for source, target in ((delta_ref, delta_hbm), (mla_ref, mla_hbm)):
+        step = source.shape[0] // PIECES
+        for i in range(PIECES):
+            part = pl.ds(i * step, step)
+            copies.append(
+                pltpu.make_async_copy(source.at[part], target.at[part], sem.at[len(copies)])
+            )
+    for copy in copies:
+        copy.start()
+    for copy in copies:
+        copy.wait()
 
 
 def solution(mesh):
@@ -471,7 +520,7 @@
         side_copies = (SPAN // 2 + 1) * (head_devices - 1)
         inputs = (query_vec, key_vec, value_vec, log_decay, beta.T, latent, latent_query, w_uv, doc_lengths.reshape(1, -1))
         inputs = [pltpu.with_memory_space_constraint(x, pltpu.HBM) for x in inputs]
-        return pl.pallas_call(
+        delta, mla = pl.pallas_call(
             functools.partial(body, shards, head_devices, heads, WIDTH**-0.5),
             out_shape=(
                 jax.ShapeDtypeStruct((rows, width), F32),
@@ -497,11 +546,11 @@
                 pltpu.VMEM((heads,) + square, F32),
                 pltpu.VMEM((heads,) + square, BF16),
                 pltpu.VMEM((heads,) + square, BF16),
-                pltpu.VMEM((5, heads) + square, BF16),
-                pltpu.VMEM((5, heads) + square, BF16),
+                pltpu.VMEM((6, heads) + square, BF16),
+                pltpu.VMEM((6, heads) + square, BF16),
                 dma((8 + heads,)),
-                dma((5, heads // BATCH)),
-                dma((5, heads // BATCH)),
+                dma((6, heads // BATCH)),
+                dma((6, heads // BATCH)),
                 dma((2,)),
                 dma((2,)),
                 dma((side_copies,)),
@@ -515,6 +564,19 @@
             cost_estimate=pl.CostEstimate(flops=3_000_000_000, bytes_accessed=6_000_000, transcendentals=1_000_000),
             name="packed_attention",
         )(*inputs)
+        anywhere = pl.BlockSpec(memory_space=pl.ANY)
+        return pl.pallas_call(
+            write_out,
+            out_shape=(
+                jax.ShapeDtypeStruct((rows, width), F32),
+                jax.ShapeDtypeStruct((rows, width), BF16),
+            ),
+            in_specs=[anywhere, anywhere],
+            out_specs=(pl.BlockSpec(memory_space=pltpu.HBM), pl.BlockSpec(memory_space=pltpu.HBM)),
+            scratch_shapes=[dma((2 * PIECES,))],
+            compiler_params=pltpu.CompilerParams(vmem_limit_bytes=1024 * 1024),
+            name="write_out",
+        )(delta, mla)
 
     return jax.shard_map(
         step,

time: 26.4 us -> 25.3 us (0.958); the launches traced: 26.1 us -> 25.3 us
  local copies, waits for them, and re-layouts: 1.5 us -> 0 us
  Pallas kernels: 23.9 us -> 24.6 us
    unnamed x2 -> x0, local copies, waits for them, and re-layouts: 1.5 us -> none
    pallas_call x0 -> x1, Pallas kernels: none -> 0.91 us  [step(): pl.pallas_call(write_out, out_shape=(jax.ShapeDtypeStruct((rows, width),...]
where the time goes in v5:
time: 25.3 us
  Pallas kernels  24.6 us (97%)
  between operations  0.64 us (3%)
    pallas_call x1, Pallas kernels, step(): pl.pallas_call(functools.partial(body, shards, head_devices, heads, WIDTH...  23.7 us
    pallas_call x1, Pallas kernels, step(): pl.pallas_call(write_out, out_shape=(jax.ShapeDtypeStruct((rows, width),...  0.91 us

profile of v5, /device:TPU:7, one launch (start us, length us, event | category | flops | bytes accessed | tf_op | source)
XLA Modules:
  0.0 25.3 jit_solution(10969900496934369771)
XLA Ops:
  0.6 23.7 %packed_attention.1 = (f32[128,1024]{1,0:T(8,128)S(1)}, bf16[128,1024]{1,0:T(8,128)(2,1)S(1)}) custom-call(f32[128,1024]{1,0:T(8,128)} %query_hbm.1, f32[128,1024]{1,0:T(8,128)} %key_hbm.1, f32[128,1024]{1,0:T(8,128)} %value_hbm.1, f32[128,1024]{1,0:T(8,128)} %decay_hbm.1, f32[8,128]{1,0:T(8,128)} %bitcast.2, bf16[32,512]{1,0:T(8,128)(2,1)} %latent_hbm.1, ...), custom_call_target="tpu_custom_call" | custom-call | flops 3000000000 | bytes 6000000 | tf_op jit(solution)/shard_map/packed_attention/pallas_call | solution.py:523
  24.4 0.9 %write_out.1 = (f32[128,1024]{1,0:T(8,128)}, bf16[128,1024]{1,0:T(8,128)(2,1)}) custom-call(f32[128,1024]{1,0:T(8,128)S(1)} %get-tuple-element.4.delta_ref, bf16[128,1024]{1,0:T(8,128)(2,1)S(1)} %get-tuple-element.5.mla_ref), custom_call_target="tpu_custom_call" | custom-call | tf_op jit(solution)/shard_map/write_out/pallas_call | solution.py:568

commit v6 on v5

--- a/solution.py
+++ b/solution.py
@@ -160,11 +160,12 @@
         left_ref[h] = (query * part["in_scale"] - output[:, WIDTH:]).astype(BF16)
 
 
-def latent_part(first, heads, scale, query_rows, keys, bias, up_ref, out_ref):
-    rows = heads * TOK
-    scores = mul_nt(query_rows[first * TOK : first * TOK + rows, :], keys[...])
-    mask = jnp.concatenate([bias[...]] * heads, axis=0)
-    scores = scores * scale + mask
+def latent_scores(first, heads, scale, query_rows, keys, bias):
+    rows = query_rows[first * TOK : (first + heads) * TOK, :]
+    return mul_nt(rows, keys[...]) * scale + jnp.concatenate([bias[...]] * heads, axis=0)
+
+
+def latent_finish(first, heads, scores, keys, up_ref, out_ref):
     top = jnp.max(scores, axis=1, keepdims=True)
     weights = jnp.exp(scores - top)
     totals = jnp.sum(weights, axis=1, keepdims=True)
@@ -415,10 +416,9 @@
     for i in range(2):
         twin_copy(i).wait_recv()
 
-    def latent_at(part):
-        latent_part(part * 4, 4, scale, latq_v, keys, bias, up_v, mla_v)
-
-    latent_at(0)
+    half = heads // 2
+    scores = [latent_scores(part * half, half, scale, latq_v, keys, bias) for part in range(2)]
+    latent_finish(0, half, scores[0], keys, up_v, mla_v)
 
     @pl.when(is_b & (chip > 1))
     def _():
@@ -426,7 +426,7 @@
             take_state(MAP_G, group)
             send_state(MAP_Y, group)
 
-    latent_at(1)
+    latent_finish(half, half, scores[1], keys, up_v, mla_v)
 
     def start_of(h):
         return recv_buf[MAP_C, h].astype(F32)

time: 25.3 us -> 24.6 us (0.972)
  Pallas kernels: 24.6 us -> 23.9 us
    pallas_call x1, Pallas kernels: 23.7 us -> 23 us  [step(): pl.pallas_call(functools.partial(body, shards, head_devices, heads, WIDTH...]
where the time goes in v6:
time: 24.6 us; the launch traced here: 24.5 us
  Pallas kernels  23.9 us (97%)
  between operations  0.64 us (3%)
    pallas_call x1, Pallas kernels, step(): pl.pallas_call(functools.partial(body, shards, head_devices, heads, WIDTH...  23 us
    pallas_call x1, Pallas kernels, step(): pl.pallas_call(write_out, out_shape=(jax.ShapeDtypeStruct((rows, width),...  0.91 us

profile of v6, /device:TPU:7, one launch (start us, length us, event | category | flops | bytes accessed | tf_op | source)
XLA Modules:
  0.0 24.5 jit_solution(10110507846641159489)
XLA Ops:
  0.6 23.0 %packed_attention.1 = (f32[128,1024]{1,0:T(8,128)S(1)}, bf16[128,1024]{1,0:T(8,128)(2,1)S(1)}) custom-call(f32[128,1024]{1,0:T(8,128)} %query_hbm.1, f32[128,1024]{1,0:T(8,128)} %key_hbm.1, f32[128,1024]{1,0:T(8,128)} %value_hbm.1, f32[128,1024]{1,0:T(8,128)} %decay_hbm.1, f32[8,128]{1,0:T(8,128)} %bitcast.2, bf16[32,512]{1,0:T(8,128)(2,1)} %latent_hbm.1, ...), custom_call_target="tpu_custom_call" | custom-call | flops 3000000000 | bytes 6000000 | tf_op jit(solution)/shard_map/packed_attention/pallas_call | solution.py:523
  23.6 0.9 %write_out.1 = (f32[128,1024]{1,0:T(8,128)}, bf16[128,1024]{1,0:T(8,128)(2,1)}) custom-call(f32[128,1024]{1,0:T(8,128)S(1)} %get-tuple-element.4.delta_ref, bf16[128,1024]{1,0:T(8,128)(2,1)S(1)} %get-tuple-element.5.mla_ref), custom_call_target="tpu_custom_call" | custom-call | tf_op jit(solution)/shard_map/write_out/pallas_call | solution.py:568

commit v7 on v6

--- a/solution.py
+++ b/solution.py
@@ -360,8 +360,10 @@
     def _():
         for group in groups:
             incoming = take_state(MAP_A, group)
+            emit(group, [recv_buf[MAP_C, h] for h in members(group)])
             for h, x in zip(members(group), incoming):
                 step_ref[h] = mul(a_ref[h], x).astype(BF16)
+                left_ref[h] = mul(left_ref[h], x).astype(BF16)
 
     for i in range(2):
         @pl.when(shard >= near[i])
@@ -411,6 +413,16 @@
     def _():
         twin_copy(0).start()
 
+    @pl.when(is_a & (chip > 0))
+    def _():
+        for group in groups:
+            emit(group, take_state(MAP_X, group))
+
+    @pl.when(is_b & (chip > 0))
+    def _():
+        for group in groups:
+            emit(group, [recv_buf[MAP_D, h] for h in members(group)])
+
     for load in loads[6:-1]:
         load.wait()
     for i in range(2):
@@ -428,44 +440,10 @@
 
     latent_finish(half, half, scores[1], keys, up_v, mla_v)
 
-    def start_of(h):
-        return recv_buf[MAP_C, h].astype(F32)
-
-    def add_out(group, incoming):
-        for h, state in zip(members(group), incoming):
-            lanes = slice(h * WIDTH, (h + 1) * WIDTH)
-            base[:, lanes] += mul(left_ref[h], state.astype(BF16))
-
-    @pl.when(is_b & (chip == 0))
-    def _():
-        for group in groups:
-            add_out(group, [recv_buf[MAP_C, h] for h in members(group)])
-
-    @pl.when(is_b & (chip == 1))
-    def _():
-        for group in groups:
-            add_out(
-                group,
-                [start_of(h) + mul(recv_buf[MAP_A, h], recv_buf[MAP_D, h]) for h in members(group)],
-            )
-
     @pl.when(is_b & (chip > 1))
     def _():
         for group in groups:
-            add_out(
-                group,
-                [
-                    start_of(h)
-                    + mul(recv_buf[MAP_A, h], recv_buf[MAP_D, h])
-                    + mul(recv_buf[MAP_A, h], recv_buf[MAP_G, h])
-                    for h in members(group)
-                ],
-            )
-
-    @pl.when(is_a & (chip > 0))
-    def _():
-        for group in groups:
-            emit(group, take_state(MAP_X, group))
+            emit(group, [recv_buf[MAP_G, h] for h in members(group)])
 
     @pl.when(is_a & (chip > 1))
     def _():

time: 24.6 us -> 24.2 us (0.984)
  Pallas kernels: 23.9 us -> 23.5 us
    pallas_call x1, Pallas kernels: 23 us -> 22.6 us  [step(): pl.pallas_call(functools.partial(body, shards, head_devices, heads, WIDTH...]
where the time goes in v7:
time: 24.2 us
  Pallas kernels  23.5 us (97%)
  between operations  0.64 us (3%)
    pallas_call x1, Pallas kernels, step(): pl.pallas_call(functools.partial(body, shards, head_devices, heads, WIDTH...  22.6 us
    pallas_call x1, Pallas kernels, step(): pl.pallas_call(write_out, out_shape=(jax.ShapeDtypeStruct((rows, width),...  0.91 us

profile of v7, /device:TPU:7, one launch (start us, length us, event | category | flops | bytes accessed | tf_op | source)
XLA Modules:
  0.0 24.2 jit_solution(16260116520974468474)
XLA Ops:
  0.6 22.6 %packed_attention.1 = (f32[128,1024]{1,0:T(8,128)S(1)}, bf16[128,1024]{1,0:T(8,128)(2,1)S(1)}) custom-call(f32[128,1024]{1,0:T(8,128)} %query_hbm.1, f32[128,1024]{1,0:T(8,128)} %key_hbm.1, f32[128,1024]{1,0:T(8,128)} %value_hbm.1, f32[128,1024]{1,0:T(8,128)} %decay_hbm.1, f32[8,128]{1,0:T(8,128)} %bitcast.2, bf16[32,512]{1,0:T(8,128)(2,1)} %latent_hbm.1, ...), custom_call_target="tpu_custom_call" | custom-call | flops 3000000000 | bytes 6000000 | tf_op jit(solution)/shard_map/packed_attention/pallas_call | solution.py:501
  23.2 0.9 %write_out.1 = (f32[128,1024]{1,0:T(8,128)}, bf16[128,1024]{1,0:T(8,128)(2,1)}) custom-call(f32[128,1024]{1,0:T(8,128)S(1)} %get-tuple-element.4.delta_ref, bf16[128,1024]{1,0:T(8,128)(2,1)S(1)} %get-tuple-element.5.mla_ref), custom_call_target="tpu_custom_call" | custom-call | tf_op jit(solution)/shard_map/write_out/pallas_call | solution.py:546

commit v8 on v7

--- a/solution.py
+++ b/solution.py
@@ -16,7 +16,7 @@
 TOK = 128
 WIDTH = 128
 LEVELS = 7
-BATCH = 4
+BATCH = 2
 PIECES = 2
 
 
@@ -26,10 +26,6 @@
 
 def mul_nt(left, right):
     return lax.dot_general(left, right, (((1,), (1,)), ((), ())), preferred_element_type=F32)
-
-
-def mul_tn(left, right):
-    return lax.dot_general(left, right, (((0,), (0,)), ((), ())), preferred_element_type=F32)
 
 
 def halves(matrix):
@@ -116,7 +112,7 @@
                 right=jnp.concatenate(
                     [value_ref[:, lanes] * beta, key_grow * in_scale * beta], axis=1
                 ),
-                tail=halves(key_shrink * (tail * to_end)),
+                tail=halves((key_shrink * (tail * to_end)).T),
                 end=jnp.exp(end) * link_last,
             )
         )
@@ -140,7 +136,7 @@
     solved = [halves(solved[h] + mul(inverse[h], rest[h].astype(BF16))) for h in span]
     for group in range(len(parts) // BATCH):
         for h in range(group * BATCH, (group + 1) * BATCH):
-            change = three(mul_tn, parts[h]["tail"], solved[h])
+            change = three(mul, parts[h]["tail"], solved[h])
             c_ref[h] = change[:, :WIDTH]
             a_ref[h] = (jnp.where(row == col, parts[h]["end"], 0.0) - change[:, WIDTH:]).astype(BF16)
         finished(group)

time: 24.2 us -> 24.7 us (1.021)
  the two profiles are of different devices: /device:TPU:7 before, /device:TPU:6 now
where the time goes in v8:
time: 24.7 us; the launch traced here: 24.6 us
  Pallas kernels  24 us (97%)
  between operations  0.64 us (3%)
    pallas_call x1, Pallas kernels, step(): pl.pallas_call(functools.partial(body, shards, head_devices, heads, WIDTH...  23.1 us
    pallas_call x1, Pallas kernels, step(): pl.pallas_call(write_out, out_shape=(jax.ShapeDtypeStruct((rows, width),...  0.91 us

profile of v8, /device:TPU:6, one launch (start us, length us, event | category | flops | bytes accessed | tf_op | source)
XLA Modules:
  0.0 24.6 jit_solution(13272252473687310969)
XLA Ops:
  0.6 23.1 %packed_attention.1 = (f32[128,1024]{1,0:T(8,128)S(1)}, bf16[128,1024]{1,0:T(8,128)(2,1)S(1)}) custom-call(f32[128,1024]{1,0:T(8,128)} %query_hbm.1, f32[128,1024]{1,0:T(8,128)} %key_hbm.1, f32[128,1024]{1,0:T(8,128)} %value_hbm.1, f32[128,1024]{1,0:T(8,128)} %decay_hbm.1, f32[8,128]{1,0:T(8,128)} %bitcast.2, bf16[32,512]{1,0:T(8,128)(2,1)} %latent_hbm.1, ...), custom_call_target="tpu_custom_call" | custom-call | flops 3000000000 | bytes 6000000 | tf_op jit(solution)/shard_map/packed_attention/pallas_call | solution.py:497
  23.7 0.9 %write_out.1 = (f32[128,1024]{1,0:T(8,128)}, bf16[128,1024]{1,0:T(8,128)(2,1)}) custom-call(f32[128,1024]{1,0:T(8,128)S(1)} %get-tuple-element.4.delta_ref, bf16[128,1024]{1,0:T(8,128)(2,1)S(1)} %get-tuple-element.5.mla_ref), custom_call_target="tpu_custom_call" | custom-call | tf_op jit(solution)/shard_map/write_out/pallas_call | solution.py:542
